TPU v7x, 256 devices: a whole 4x4x8 slice. The times are simulated.
256 devices in a mesh: vis: 32 (over x_hi, z, core), facet: 8 (over y, x_lo).
Axes of the slice: x: 4 (x_hi: 2, x_lo: 2; x = x_hi * 2 + x_lo), y: 4, z: 8, core: 2. Of those that a mesh axis runs over, the one named last changes fastest.
Arguments:
- visibilities: float32 [8, 16384], P(None, 'vis'), may hold values from -6 to 6
- weights: float32 [16384], P('vis'), may hold values from 0.5 to 2
- live_slots: int32 [16384], P('vis'), may hold values from 0 to 1, as said below
- station_p: int32 [16384], P('vis'), may hold values from 0 to 61
- station_q: int32 [16384], P('vis'), may hold values from 0 to 61
- interval: int32 [16384], P('vis'), may hold values from 0 to 127
- cell_row: int32 [16384], replicated, may hold values from 0 to 63
- cell_col: int32 [16384], replicated, may hold values from 0 to 2047
- jones_gains: float32 [8, 8, 128, 62], P('facet', None, 'vis'), may hold values from -1.5 to 1.5
- model_image: float32 [8, 2048, 2048], P('facet', 'vis'), may hold values from -6 to 6
Outputs:
- residual_vis: float32 [8, 16384], P(None, 'vis')
- dirty_image: float32 [8, 2048, 2048], P('facet', 'vis')
Inputs may be any that keep to these rules, and one draw needn't show every extreme that they name: `live_slots`: each device's slots are ordered by tile owner, 16 slots an owner, live ones first; in every draw one tile owner receives 16 live slots from every device.
All inputs are finite; a program needn't handle non-finite values.
Results may differ from a plain program's by a relative error of at most 0.00011.
Values sent between devices are 32-bit elements; how exact they have to be, the bound alone decides.
A program may use at most 192 MiB of HBM per device.

v0:
```python
import functools
import math

import jax
import jax.numpy as jnp
import numpy as np
from jax import lax
from jax.experimental import pallas as pl
from jax.experimental.pallas import tpu as pltpu
from jax.sharding import PartitionSpec as P

TWO_PI = 2.0 * math.pi
MESH = pl.DeviceIdType.MESH
F32 = jnp.float32
BF16 = jnp.bfloat16

RADIX = 16
INNER = 128
SIDE = RADIX * INNER


def split_table(table):
    high = table.astype(BF16)
    low = (table - high.astype(np.float64)).astype(BF16)
    return high, low


def make_tables():
    inner = np.arange(INNER)
    angle = TWO_PI * (np.outer(inner, inner) % INNER) / INNER
    first = np.concatenate([np.cos(angle), -np.sin(angle)], axis=1)
    last = np.concatenate([np.cos(angle), -np.sin(angle)], axis=0)
    twist = TWO_PI * np.outer(np.arange(RADIX), inner) / SIDE
    twist = np.stack([np.cos(twist), np.sin(twist)]).astype(np.float32)
    return split_table(first) + split_table(last) + (twist,)


def split_pair(value):
    high = value.astype(BF16)
    low = (value - high.astype(F32)).astype(BF16)
    return high, low


def matmul(left, right):
    return jnp.dot(left, right, preferred_element_type=F32)


def cmul_const(pair, real, imag):
    re, im = pair
    return re * real - im * imag, re * imag + im * real


def radix4(vals, sign):
    (ar, ai), (br, bi), (cr, ci), (dr, di) = vals
    sr, si = ar + cr, ai + ci
    tr, ti = ar - cr, ai - ci
    ur, ui = br + dr, bi + di
    wr, wi = br - dr, bi - di
    if sign < 0:
        xr, xi = wi, -wr
    else:
        xr, xi = -wi, wr
    return [(sr + ur, si + ui), (tr + xr, ti + xi), (sr - ur, si - ui), (tr - xr, ti - xi)]


def radix16(vals, sign):
    inner = [radix4([vals[4 * n1 + n2] for n1 in range(4)], sign) for n2 in range(4)]
    out = [None] * 16
    for k1 in range(4):
        column = []
        for n2 in range(4):
            turn = n2 * k1
            value = inner[n2][k1]
            if turn == 4:
                re, im = value
                value = (im, -re) if sign < 0 else (-im, re)
            elif turn == 2 or turn == 6:
                half = math.sqrt(0.5)
                re, im = value
                if sign < 0:
                    value = ((re + im) * half, (im - re) * half)
                else:
                    value = ((re - im) * half, (re + im) * half)
                if turn == 6:
                    re, im = value
                    value = (im, -re) if sign < 0 else (-im, re)
            elif turn:
                angle = sign * TWO_PI * turn / 16
                value = cmul_const(value, math.cos(angle), math.sin(angle))
            column.append(value)
        for k2, value in enumerate(radix4(column, sign)):
            out[k1 + 4 * k2] = value
    return out


def unit_phase(step):
    quarter = (step + 256) >> 9
    angle = (step - (quarter << 9)).astype(F32) * (TWO_PI / SIDE)
    square = angle * angle
    sine = angle * (
        1.0
        + square
        * (-1.0 / 6 + square * (1.0 / 120 + square * (-1.0 / 5040 + square * (1.0 / 362880))))
    )
    cosine = 1.0 + square * (
        -0.5 + square * (1.0 / 24 + square * (-1.0 / 720 + square * (1.0 / 40320)))
    )
    odd = (quarter & 1) == 1
    cos_mag = jnp.where(odd, sine, cosine)
    sin_mag = jnp.where(odd, cosine, sine)
    cos_val = jnp.where(((quarter + 1) & 2) == 2, -cos_mag, cos_mag)
    sin_val = jnp.where((quarter & 2) == 2, -sin_mag, sin_mag)
    return cos_val, sin_val


def lane_block(shape):
    return lax.broadcasted_iota(jnp.int32, shape, 1) >> 5


def slots_to_pairs(read_block, group):
    blocks = [read_block(4 * group + member) for member in range(4)]
    where = lane_block(blocks[0].shape)
    rows = []
    for turn in range(4):
        total = None
        for member in range(4):
            shift = 32 * (member - turn) % 128
            moved = pltpu.roll(blocks[member], shift, 1) if shift else blocks[member]
            total = moved if total is None else jnp.where(where == member, moved, total)
        rows.append(total)
    return rows


def pairs_to_slots(rows):
    where = lane_block(rows[0].shape)
    blocks = []
    for member in range(4):
        total = None
        for turn in range(4):
            shift = 32 * (turn - member) % 128
            moved = pltpu.roll(rows[turn], shift, 1) if shift else rows[turn]
            total = moved if total is None else jnp.where(where == turn, moved, total)
        blocks.append(total)
    return blocks


def wide_row(block):
    return jnp.concatenate([block[k : k + 1, :] for k in range(4)], axis=1)


def tall_block(row):
    return jnp.concatenate([row[:, 128 * k : 128 * (k + 1)] for k in range(4)], axis=0)


def jones_outer(left, right):
    real_rows = []
    imag_rows = []
    for row_a in range(2):
        for row_b in range(2):
            real_sum = 0.0
            imag_sum = 0.0
            for inner in range(2):
                left_re = left[row_a * 2 + inner]
                left_im = left[4 + row_a * 2 + inner]
                right_re = right[row_b * 2 + inner]
                right_im = right[4 + row_b * 2 + inner]
                real_sum = real_sum + left_re * right_re + left_im * right_im
                imag_sum = imag_sum + left_im * right_re - left_re * right_im
            real_rows.append(real_sum)
            imag_rows.append(imag_sum)
    return jnp.concatenate(real_rows, axis=0), jnp.concatenate(imag_rows, axis=0)


def jones_stokes(left, right, resid):
    total_re = 0.0
    total_im = 0.0
    for inner in range(2):
        for row_a in range(2):
            for row_b in range(2):
                left_re = left[row_a * 2 + inner]
                left_im = left[4 + row_a * 2 + inner]
                res_re = resid[row_a * 2 + row_b]
                res_im = resid[4 + row_a * 2 + row_b]
                right_re = right[row_b * 2 + inner]
                right_im = right[4 + row_b * 2 + inner]
                mid_re = left_re * res_re + left_im * res_im
                mid_im = left_re * res_im - left_im * res_re
                total_re = total_re + mid_re * right_re - mid_im * right_im
                total_im = total_im + mid_re * right_im + mid_im * right_re
    return 0.5 * total_re, 0.5 * total_im


def kernel(
    n_vis,
    n_facet,
    vis_ref,
    weight_ref,
    live_ref,
    station_p_ref,
    station_q_ref,
    interval_ref,
    cell_row_ref,
    cell_col_ref,
    gain_ref,
    image_ref,
    first_hi_ref,
    first_lo_ref,
    last_hi_ref,
    last_lo_ref,
    twist_ref,
    resid_ref,
    dirty_ref,
    gain_all,
    part_out,
    part_in,
    pred_in,
    stokes_in,
    lines,
    work_re,
    work_im,
    table,
    cells,
    values,
    block_cos,
    block_sin,
    fine_cos,
    fine_sin,
    gain_send,
    gain_recv,
    part_send,
    part_recv,
    pred_send,
    pred_recv,
    stokes_send,
    stokes_recv,
):
    me = lax.axis_index("vis")
    facet = lax.axis_index("facet")
    side_x = image_ref.shape[0]

    def vis_peer(step):
        return lax.rem(me + step, n_vis)

    def facet_peer(step):
        return lax.rem(facet + step, n_facet)

    barrier = pltpu.get_barrier_semaphore()

    def greet_vis(step, carry):
        pl.semaphore_signal(barrier, 1, device_id=(vis_peer(step), facet), device_id_type=MESH)
        return carry

    def greet_facet(step, carry):
        pl.semaphore_signal(barrier, 1, device_id=(me, facet_peer(step)), device_id_type=MESH)
        return carry

    lax.fori_loop(1, n_vis, greet_vis, 0)
    lax.fori_loop(1, n_facet, greet_facet, 0)

    def send_all(source, target, send_sem, recv_sem):
        def send(step, carry):
            pltpu.make_async_remote_copy(
                src_ref=source(vis_peer(step)),
                dst_ref=target.at[me],
                send_sem=send_sem,
                recv_sem=recv_sem,
                device_id=(vis_peer(step), facet),
                device_id_type=MESH,
            ).start()
            return carry

        lax.fori_loop(1, n_vis, send, 0)

    def wait_blocks(buffer, count, sem):
        view = buffer.at[pl.ds(0, count)]
        pltpu.make_async_copy(view, view, sem).wait()

    intervals_here = gain_ref.shape[1]
    stations = gain_ref.shape[2]
    gain_all[me] = jnp.zeros((8, 256), F32)
    for comp in range(8):
        half, lane = comp // 4, 64 * (comp % 4)
        gain_all[me, 4 * half : 4 * half + intervals_here, lane : lane + stations] = gain_ref[comp]

    pl.semaphore_wait(barrier, n_vis + n_facet - 2)
    send_all(lambda peer: gain_all.at[me], gain_all, gain_send, gain_recv)

    lines[...] = image_ref[...].T
    for b in range(RADIX):
        part = lines[pl.ds(b, INNER, stride=RADIX), :].T
        high, low = split_pair(part)
        both = matmul(high, first_hi_ref[...]) + (
            matmul(high, first_lo_ref[...]) + matmul(low, first_hi_ref[...])
        )
        re, im = both[:, :INNER], both[:, INNER:]
        cos = twist_ref[0, b : b + 1, :]
        sin = twist_ref[1, b : b + 1, :]
        work_re[b] = re * cos + im * sin
        work_im[b] = im * cos - re * sin

    def forward_rows(chunk, carry):
        rows = pl.ds(pl.multiple_of(chunk * 8, 8), 8)
        rows_im = pl.ds(pl.multiple_of(side_x + chunk * 8, 8), 8)
        vals = radix16([(work_re[b, rows, :], work_im[b, rows, :]) for b in range(RADIX)], -1.0)
        for q in range(RADIX):
            table[q, rows, :] = vals[q][0]
            table[q, rows_im, :] = vals[q][1]
        return carry

    lax.fori_loop(0, side_x // 8, forward_rows, 0)

    def order_cells(group, carry):
        lanes = pl.ds(pl.multiple_of(group * 128, 128), 128)

        def read(holder):
            rows = pl.ds(holder * 4, 4)
            return jnp.concatenate([cell_row_ref[rows, :], cell_col_ref[rows, :]], axis=0)

        for turn, rows in enumerate(slots_to_pairs(read, group)):
            cells[8 * turn : 8 * turn + 8, lanes] = rows
        return carry

    lax.fori_loop(0, n_vis // 4, order_cells, 0)

    width = cells.shape[1]
    chunk_w = 256

    def pair_row(pair):
        return lax.rem(pair, 4) * 8 + pair // 4

    def one_hot(pair, lanes):
        local = cells[pl.ds(pair_row(pair), 1), lanes]
        lane = lax.broadcasted_iota(jnp.int32, local.shape, 1)
        local = local + ((lane >> 4) & 1) * 64
        index = lax.broadcasted_iota(jnp.int32, (INNER, local.shape[1]), 0)
        return jnp.where(index == local, 1.0, 0.0).astype(BF16)

    def forward_pair(pair, carry):
        column = cells[pl.ds(pair_row(pair) + 4, 1), :]
        index = lax.broadcasted_iota(jnp.int32, (8, width), 0)
        cos, sin = unit_phase((column * (me * side_x + 8 * index)) & (SIDE - 1))
        block_cos[pair] = cos
        block_sin[pair] = sin
        cos, sin = unit_phase((column * index) & (SIDE - 1))
        fine_cos[pair] = cos
        fine_sin[pair] = sin
        high, low = split_pair(table[pair])
        both = jnp.concatenate([high, low], axis=0)
        for start in range(0, width, chunk_w):
            lanes = slice(start, start + chunk_w)
            picked = matmul(both, one_hot(pair, lanes))
            picked = picked[: 2 * side_x] + picked[2 * side_x :]
            sum_re = 0.0
            sum_im = 0.0
            for block in range(side_x // 8):
                re = picked[8 * block : 8 * block + 8]
                im = picked[side_x + 8 * block : side_x + 8 * block + 8]
                cos = block_cos[pair, block : block + 1, lanes]
                sin = block_sin[pair, block : block + 1, lanes]
                sum_re = sum_re + (re * cos + im * sin)
                sum_im = sum_im + (im * cos - re * sin)
            cos = fine_cos[pair, :, lanes]
            sin = fine_sin[pair, :, lanes]
            out_re = jnp.sum(sum_re * cos + sum_im * sin, axis=0, keepdims=True)
            out_im = jnp.sum(sum_im * cos - sum_re * sin, axis=0, keepdims=True)
            values[pl.ds(pair_row(pair), 1), lanes] = out_re
            values[pl.ds(pair_row(pair) + 4, 1), lanes] = out_im
        return carry

    lax.fori_loop(0, RADIX, forward_pair, 0)

    def pack_values(group, carry):
        lanes = pl.ds(pl.multiple_of(group * 128, 128), 128)
        rows = [values[8 * turn : 8 * turn + 8, lanes] for turn in range(4)]
        for member, block in enumerate(pairs_to_slots(rows)):
            part_out[4 * group + member] = block
        return carry

    lax.fori_loop(0, n_vis // 4, pack_values, 0)
    send_all(lambda peer: part_out.at[peer], part_in, part_send, part_recv)
    part_in[me] = part_out[me]

    wait_blocks(gain_all, n_vis - 1, gain_recv)
    high, low = split_pair(gain_all[...].reshape(n_vis * 8, 256).T)
    both = jnp.concatenate([high, low], axis=0)
    interval = wide_row(interval_ref[...])
    gain_row = (interval >> 2) * 8 + (interval & 3)
    station_p = wide_row(station_p_ref[...])
    station_q = wide_row(station_q_ref[...])
    slots = interval.shape[1]
    station = lax.broadcasted_iota(jnp.int32, (64, slots), 0)
    at_p = jnp.where(station == station_p, 1.0, 0.0)
    at_q = jnp.where(station == station_q, 1.0, 0.0)
    index = lax.broadcasted_iota(jnp.int32, (n_vis * 8, slots), 0)
    jones_p = []
    jones_q = []
    for half in range(2):
        hot = jnp.where(index == gain_row + 4 * half, 1.0, 0.0).astype(BF16)
        picked = matmul(both, hot)
        picked = picked[:256] + picked[256:]
        for comp in range(4):
            here = picked[64 * comp : 64 * comp + 64]
            jones_p.append(jnp.sum(here * at_p, axis=0, keepdims=True))
            jones_q.append(jnp.sum(here * at_q, axis=0, keepdims=True))
    outer_re, outer_im = jones_outer(jones_p, jones_q)
    live = wide_row(live_ref[...]).astype(F32)
    scale = wide_row(weight_ref[...]) * live

    wait_blocks(part_in, n_vis - 1, part_recv)
    model = jnp.sum(part_in[...], axis=0) * (1.0 / SIDE)
    model_re = wide_row(model[0:4])
    model_im = wide_row(model[4:8])
    pred_in[facet, 0:4, :] = model_re * outer_re - model_im * outer_im
    pred_in[facet, 4:8, :] = model_re * outer_im + model_im * outer_re

    def send_pred(step, carry):
        pltpu.make_async_remote_copy(
            src_ref=pred_in.at[facet],
            dst_ref=pred_in.at[facet],
            send_sem=pred_send,
            recv_sem=pred_recv,
            device_id=(me, facet_peer(step)),
            device_id_type=MESH,
        ).start()
        return carry

    lax.fori_loop(1, n_facet, send_pred, 0)
    wait_blocks(pred_in, n_facet - 1, pred_recv)
    predicted = pred_in[0]
    for other in range(1, n_facet):
        predicted = predicted + pred_in[other]
    resid = (vis_ref[...] - predicted) * live
    resid_ref[...] = resid
    stokes_re, stokes_im = jones_stokes(jones_p, jones_q, [resid[c : c + 1] for c in range(8)])
    stokes_in[me, 0:4, :] = tall_block(stokes_re * scale)
    stokes_in[me, 4:8, :] = tall_block(stokes_im * scale)
    send_all(lambda peer: stokes_in.at[me], stokes_in, stokes_send, stokes_recv)
    wait_blocks(stokes_in, n_vis - 1, stokes_recv)

    def order_stokes(group, carry):
        lanes = pl.ds(pl.multiple_of(group * 128, 128), 128)
        for turn, rows in enumerate(slots_to_pairs(lambda holder: stokes_in[holder], group)):
            values[8 * turn : 8 * turn + 8, lanes] = rows
        return carry

    lax.fori_loop(0, n_vis // 4, order_stokes, 0)

    def backward_pair(pair, carry):
        total = jnp.zeros((4 * side_x, INNER), F32)
        for start in range(0, width, chunk_w):
            lanes = slice(start, start + chunk_w)
            re = values[pl.ds(pair_row(pair), 1), lanes]
            im = values[pl.ds(pair_row(pair) + 4, 1), lanes]
            cos = fine_cos[pair, :, lanes]
            sin = fine_sin[pair, :, lanes]
            fine_re = re * cos - im * sin
            fine_im = re * sin + im * cos
            real_rows = []
            imag_rows = []
            for block in range(side_x // 8):
                cos = block_cos[pair, block : block + 1, lanes]
                sin = block_sin[pair, block : block + 1, lanes]
                real_rows.append(fine_re * cos - fine_im * sin)
                imag_rows.append(fine_re * sin + fine_im * cos)
            high, low = split_pair(jnp.concatenate(real_rows + imag_rows, axis=0))
            both = jnp.concatenate([high, low], axis=0)
            total = total + lax.dot_general(
                both,
                one_hot(pair, lanes),
                (((1,), (1,)), ((), ())),
                preferred_element_type=F32,
            )
        table[pair] = total[: 2 * side_x] + total[2 * side_x :]
        return carry

    lax.fori_loop(0, RADIX, backward_pair, 0)

    def backward_rows(chunk, carry):
        rows = pl.ds(pl.multiple_of(chunk * 8, 8), 8)
        rows_im = pl.ds(pl.multiple_of(side_x + chunk * 8, 8), 8)
        vals = radix16([(table[q, rows, :], table[q, rows_im, :]) for q in range(RADIX)], 1.0)
        for b in range(RADIX):
            re, im = vals[b]
            cos = twist_ref[0, b : b + 1, :]
            sin = twist_ref[1, b : b + 1, :]
            work_re[b, rows, :] = re * cos - im * sin
            work_im[b, rows, :] = re * sin + im * cos
        return carry

    lax.fori_loop(0, side_x // 8, backward_rows, 0)

    factor = 4.0 / math.sqrt(slots * n_vis)
    for b in range(RADIX):
        high, low = split_pair(jnp.concatenate([work_re[b], work_im[b]], axis=1))
        part = matmul(high, last_hi_ref[...]) + (
            matmul(high, last_lo_ref[...]) + matmul(low, last_hi_ref[...])
        )
        lines[pl.ds(b, INNER, stride=RADIX), :] = (part * factor).T
    dirty_ref[...] = lines[...].T

    wait_blocks(gain_all, n_vis - 1, gain_send)
    wait_blocks(part_in, n_vis - 1, part_send)
    wait_blocks(pred_in, n_facet - 1, pred_send)
    wait_blocks(stokes_in, n_vis - 1, stokes_send)


def per_device(
    visibilities,
    weights,
    live_slots,
    station_p,
    station_q,
    interval,
    cell_row,
    cell_col,
    jones_gains,
    model_image,
):
    n_vis = lax.axis_size("vis")
    n_facet = lax.axis_size("facet")
    side_x = model_image.shape[1]
    slots = visibilities.shape[1]
    width = n_vis * slots // RADIX

    def rows_of(array):
        return array.reshape(-1, 128)

    tables = [jnp.asarray(table) for table in make_tables()]
    vmem = pl.BlockSpec(memory_space=pltpu.VMEM)
    resid, dirty = pl.pallas_call(
        functools.partial(kernel, n_vis, n_facet),
        out_shape=(
            jax.ShapeDtypeStruct((8, slots), F32),
            jax.ShapeDtypeStruct((side_x, SIDE), F32),
        ),
        in_specs=[vmem] * 15,
        out_specs=(vmem, vmem),
        scratch_shapes=[
            pltpu.VMEM((n_vis, 8, 256), F32),
            pltpu.VMEM((n_vis, 8, 128), F32),
            pltpu.VMEM((n_vis, 8, 128), F32),
            pltpu.VMEM((n_facet, 8, slots), F32),
            pltpu.VMEM((n_vis, 8, 128), F32),
            pltpu.VMEM((SIDE, side_x), F32),
            pltpu.VMEM((RADIX, side_x, INNER), F32),
            pltpu.VMEM((RADIX, side_x, INNER), F32),
            pltpu.VMEM((RADIX, 2 * side_x, INNER), F32),
            pltpu.VMEM((32, width), jnp.int32),
            pltpu.VMEM((32, width), F32),
            pltpu.VMEM((RADIX, 8, width), F32),
            pltpu.VMEM((RADIX, 8, width), F32),
            pltpu.VMEM((RADIX, 8, width), F32),
            pltpu.VMEM((RADIX, 8, width), F32),
        ]
        + [pltpu.SemaphoreType.DMA(())] * 8,
        compiler_params=pltpu.CompilerParams(
            collective_id=0, has_side_effects=True, vmem_limit_bytes=40 * 1024 * 1024
        ),
    )(
        visibilities,
        rows_of(weights),
        rows_of(live_slots),
        rows_of(station_p),
        rows_of(station_q),
        rows_of(interval),
        rows_of(cell_row),
        rows_of(cell_col),
        jones_gains[0],
        model_image[0],
        *tables,
    )
    return resid, dirty[None]


def solution(mesh):
    return jax.shard_map(
        per_device,
        mesh=mesh,
        in_specs=(
            P(None, "vis"),
            P("vis"),
            P("vis"),
            P("vis"),
            P("vis"),
            P("vis"),
            P(),
            P(),
            P("facet", None, "vis", None),
            P("facet", "vis", None),
        ),
        out_specs=(P(None, "vis"), P("facet", "vis", None)),
        check_vma=False,
    )
```

profile of v0, /device:TPU:1, one launch (start us, length us, event | category | flops | bytes accessed | tf_op | source)
XLA Modules:
  0.0 60.2 jit_solution(2630012515290493786)
XLA Ops:
  0.6 0.0 copy-start.7
  0.6 0.7 %copy-done.7 = f32[8,512]{1,0:T(8,128)S(1)} copy-done((f32[8,512]{1,0:T(8,128)S(1)}, f32[8,512]{1,0:T(8,128)}, u32[]{:S(2)}) %copy-start.7) | copy-done | bytes 16408
  1.4 0.0 copy-start
  1.4 1.0 %copy-done = f32[1,64,2048]{2,1,0:T(8,128)S(1)} copy-done((f32[1,64,2048]{2,1,0:T(8,128)S(1)}, f32[1,64,2048]{2,1,0:T(8,128)}, u32[]{:S(2)}) %copy-start) | copy-done | bytes 524312
  2.4 0.0 copy-start.1
  2.4 0.8 %copy-done.1 = s32[16384]{0:T(1024)S(1)} copy-done((s32[16384]{0:T(1024)S(1)}, s32[16384]{0:T(1024)}, u32[]{:S(2)}) %copy-start.1) | copy-done | bytes 65560
  3.2 0.0 copy-start.2
  3.2 0.8 %copy-done.2 = s32[16384]{0:T(1024)S(1)} copy-done((s32[16384]{0:T(1024)S(1)}, s32[16384]{0:T(1024)}, u32[]{:S(2)}) %copy-start.2) | copy-done | bytes 65560
  4.1 0.0 copy-start.3
  4.1 0.8 %copy-done.3 = bf16[256,128]{1,0:T(8,128)(2,1)S(1)} copy-done((bf16[256,128]{1,0:T(8,128)(2,1)S(1)}, bf16[256,128]{1,0:T(8,128)(2,1)}, u32[]{:S(2)}) %copy-start.3) | copy-done | bytes 65560
  4.9 0.0 copy-start.4
  4.9 0.8 %copy-done.4 = bf16[256,128]{1,0:T(8,128)(2,1)S(1)} copy-done((bf16[256,128]{1,0:T(8,128)(2,1)S(1)}, bf16[256,128]{1,0:T(8,128)(2,1)}, u32[]{:S(2)}) %copy-start.4) | copy-done | bytes 65560
  5.8 0.0 copy-start.5
  5.8 0.8 %copy-done.5 = bf16[128,256]{1,0:T(8,128)(2,1)S(1)} copy-done((bf16[128,256]{1,0:T(8,128)(2,1)S(1)}, bf16[128,256]{1,0:T(8,128)(2,1)}, u32[]{:S(2)}) %copy-start.5) | copy-done | bytes 65560
  6.6 0.0 copy-start.6
  6.6 0.8 %copy-done.6 = bf16[128,256]{1,0:T(8,128)(2,1)S(1)} copy-done((bf16[128,256]{1,0:T(8,128)(2,1)S(1)}, bf16[128,256]{1,0:T(8,128)(2,1)}, u32[]{:S(2)}) %copy-start.6) | copy-done | bytes 65560
  7.4 0.0 copy-start.8
  7.4 0.7 %copy-done.8 = f32[1,8,4,62]{3,2,1,0:T(4,128)S(1)} copy-done((f32[1,8,4,62]{3,2,1,0:T(4,128)S(1)}, f32[1,8,4,62]{3,2,1,0:T(4,128)}, u32[]{:S(2)}) %copy-start.8) | copy-done | bytes 7960
  8.2 0.0 copy-start.9
  8.2 0.7 %copy-done.9 = f32[2,16,128]{2,1,0:T(8,128)S(1)} copy-done((f32[2,16,128]{2,1,0:T(8,128)S(1)}, f32[2,16,128]{2,1,0:T(8,128)}, u32[]{:S(2)}) %copy-start.9) | copy-done | bytes 16408
  8.9 0.0 copy-start.10
  8.9 0.7 %copy-done.10 = f32[512]{0:T(512)S(1)} copy-done((f32[512]{0:T(512)S(1)}, f32[512]{0:T(512)}, u32[]{:S(2)}) %copy-start.10) | copy-done | bytes 2072
  9.6 0.0 copy-start.11
  9.6 0.7 %copy-done.11 = s32[512]{0:T(512)S(1)} copy-done((s32[512]{0:T(512)S(1)}, s32[512]{0:T(512)}, u32[]{:S(2)}) %copy-start.11) | copy-done | bytes 2072
  10.2 0.0 copy-start.12
  10.2 0.7 %copy-done.12 = s32[512]{0:T(512)S(1)} copy-done((s32[512]{0:T(512)S(1)}, s32[512]{0:T(512)}, u32[]{:S(2)}) %copy-start.12) | copy-done | bytes 2072
  10.9 0.0 copy-start.13
  10.9 0.7 %copy-done.13 = s32[512]{0:T(512)S(1)} copy-done((s32[512]{0:T(512)S(1)}, s32[512]{0:T(512)}, u32[]{:S(2)}) %copy-start.13) | copy-done | bytes 2072
  11.6 0.0 copy-start.14
  11.6 0.7 %copy-done.14 = s32[512]{0:T(512)S(1)} copy-done((s32[512]{0:T(512)S(1)}, s32[512]{0:T(512)}, u32[]{:S(2)}) %copy-start.14) | copy-done | bytes 2072
  12.3 46.5 %shard_map.158 = (f32[8,512]{1,0:T(8,128)S(1)}, f32[64,2048]{1,0:T(8,128)S(1)}) custom-call(f32[8,512]{1,0:T(8,128)S(1)} %copy-done.7, f32[4,128]{1,0:T(4,128)S(1)} %bitcast.15, s32[4,128]{1,0:T(4,128)S(1)} %bitcast.16, s32[4,128]{1,0:T(4,128)S(1)} %bitcast.17, s32[4,128]{1,0:T(4,128)S(1)} %bitcast.18, s32[4,128]{1,0:T(4,128)S(1)} %bitcast.19, ...), custom_call_target="tpu_custom_call" | custom-call | tf_op jit(solution)/shard_map/pallas_call | solution.py:530
  58.8 0.6 %copy.19 = f32[8,512]{1,0:T(8,128)} copy(f32[8,512]{1,0:T(8,128)S(1)} %get-tuple-element.8) | data formatting | bytes 32768
  59.4 0.8 %copy.20 = f32[1,64,2048]{2,1,0:T(8,128)} copy(f32[1,64,2048]{2,1,0:T(8,128)S(1)} %bitcast.10) | data formatting | bytes 1048576
Async XLA Ops:
  0.6 0.7 %copy-start.7 = (f32[8,512]{1,0:T(8,128)S(1)}, f32[8,512]{1,0:T(8,128)}, u32[]{:S(2)}) copy-start(f32[8,512]{1,0:T(8,128)} %vis_ref.1) | copy-start | bytes 49156
  1.4 1.0 %copy-start = (f32[1,64,2048]{2,1,0:T(8,128)S(1)}, f32[1,64,2048]{2,1,0:T(8,128)}, u32[]{:S(2)}) copy-start(f32[1,64,2048]{2,1,0:T(8,128)} %param.24) | copy-start | bytes 1572868
  2.4 0.8 %copy-start.1 = (s32[16384]{0:T(1024)S(1)}, s32[16384]{0:T(1024)}, u32[]{:S(2)}) copy-start(s32[16384]{0:T(1024)} %param.21) | copy-start | bytes 196612
  3.2 0.8 %copy-start.2 = (s32[16384]{0:T(1024)S(1)}, s32[16384]{0:T(1024)}, u32[]{:S(2)}) copy-start(s32[16384]{0:T(1024)} %param.22) | copy-start | bytes 196612
  4.1 0.8 %copy-start.3 = (bf16[256,128]{1,0:T(8,128)(2,1)S(1)}, bf16[256,128]{1,0:T(8,128)(2,1)}, u32[]{:S(2)}) copy-start(bf16[256,128]{1,0:T(8,128)(2,1)} %constant.13.clone.last_lo_ref) | copy-start | bytes 196612
  4.9 0.8 %copy-start.4 = (bf16[256,128]{1,0:T(8,128)(2,1)S(1)}, bf16[256,128]{1,0:T(8,128)(2,1)}, u32[]{:S(2)}) copy-start(bf16[256,128]{1,0:T(8,128)(2,1)} %constant.12.clone.last_hi_ref) | copy-start | bytes 196612
  5.8 0.8 %copy-start.5 = (bf16[128,256]{1,0:T(8,128)(2,1)S(1)}, bf16[128,256]{1,0:T(8,128)(2,1)}, u32[]{:S(2)}) copy-start(bf16[128,256]{1,0:T(8,128)(2,1)} %constant.11.clone.first_lo_ref) | copy-start | bytes 196612
  6.6 0.8 %copy-start.6 = (bf16[128,256]{1,0:T(8,128)(2,1)S(1)}, bf16[128,256]{1,0:T(8,128)(2,1)}, u32[]{:S(2)}) copy-start(bf16[128,256]{1,0:T(8,128)(2,1)} %constant.10.clone.first_hi_ref) | copy-start | bytes 196612
  7.4 0.7 %copy-start.8 = (f32[1,8,4,62]{3,2,1,0:T(4,128)S(1)}, f32[1,8,4,62]{3,2,1,0:T(4,128)}, u32[]{:S(2)}) copy-start(f32[1,8,4,62]{3,2,1,0:T(4,128)} %param.23) | copy-start | bytes 23812
  8.2 0.7 %copy-start.9 = (f32[2,16,128]{2,1,0:T(8,128)S(1)}, f32[2,16,128]{2,1,0:T(8,128)}, u32[]{:S(2)}) copy-start(f32[2,16,128]{2,1,0:T(8,128)} %constant.14.clone.twist_ref) | copy-start | bytes 49156
  8.9 0.7 %copy-start.10 = (f32[512]{0:T(512)S(1)}, f32[512]{0:T(512)}, u32[]{:S(2)}) copy-start(f32[512]{0:T(512)} %param.16) | copy-start | bytes 6148
  9.6 0.7 %copy-start.11 = (s32[512]{0:T(512)S(1)}, s32[512]{0:T(512)}, u32[]{:S(2)}) copy-start(s32[512]{0:T(512)} %param.17) | copy-start | bytes 6148
  10.2 0.7 %copy-start.12 = (s32[512]{0:T(512)S(1)}, s32[512]{0:T(512)}, u32[]{:S(2)}) copy-start(s32[512]{0:T(512)} %param.18) | copy-start | bytes 6148
  10.9 0.7 %copy-start.13 = (s32[512]{0:T(512)S(1)}, s32[512]{0:T(512)}, u32[]{:S(2)}) copy-start(s32[512]{0:T(512)} %param.19) | copy-start | bytes 6148
  11.6 0.7 %copy-start.14 = (s32[512]{0:T(512)S(1)}, s32[512]{0:T(512)}, u32[]{:S(2)}) copy-start(s32[512]{0:T(512)} %param.20) | copy-start | bytes 6148
where the time goes:
time: 60.9 us; the launch traced here: 60.2 us
  Pallas kernels  46.5 us (76%)
  local copies, waits for them, and re-layouts  13 us (21%)
  between operations  0.67 us (1%)
    pallas_call x1, Pallas kernels, per_device(): pl.pallas_call(functools.partial(kernel, n_vis, n_facet), out_shape=(jax....  46.5 us
    unnamed x32, local copies, waits for them, and re-layouts  13 us

commit v1 on v0

--- a/solution.py
+++ b/solution.py
@@ -28,11 +28,10 @@
 def make_tables():
     inner = np.arange(INNER)
     angle = TWO_PI * (np.outer(inner, inner) % INNER) / INNER
-    first = np.concatenate([np.cos(angle), -np.sin(angle)], axis=1)
-    last = np.concatenate([np.cos(angle), -np.sin(angle)], axis=0)
+    turn = np.concatenate([np.cos(angle), -np.sin(angle)], axis=0)
     twist = TWO_PI * np.outer(np.arange(RADIX), inner) / SIDE
     twist = np.stack([np.cos(twist), np.sin(twist)]).astype(np.float32)
-    return split_table(first) + split_table(last) + (twist,)
+    return np.concatenate(split_table(turn), axis=0), twist
 
 
 def split_pair(value):
@@ -117,8 +116,7 @@
     return lax.broadcasted_iota(jnp.int32, shape, 1) >> 5
 
 
-def slots_to_pairs(read_block, group):
-    blocks = [read_block(4 * group + member) for member in range(4)]
+def slots_to_pairs(blocks):
     where = lane_block(blocks[0].shape)
     rows = []
     for turn in range(4):
@@ -145,11 +143,12 @@
 
 
 def wide_row(block):
-    return jnp.concatenate([block[k : k + 1, :] for k in range(4)], axis=1)
+    return jnp.concatenate([block[k : k + 1, :] for k in range(block.shape[0])], axis=1)
 
 
 def tall_block(row):
-    return jnp.concatenate([row[:, 128 * k : 128 * (k + 1)] for k in range(4)], axis=0)
+    count = row.shape[1] // 128
+    return jnp.concatenate([row[:, 128 * k : 128 * (k + 1)] for k in range(count)], axis=0)
 
 
 def jones_outer(left, right):
@@ -190,9 +189,25 @@
     return 0.5 * total_re, 0.5 * total_im
 
 
-def kernel(
+def exchange_kernel(
     n_vis,
     n_facet,
+    vis_hbm,
+    weight_hbm,
+    live_hbm,
+    station_p_hbm,
+    station_q_hbm,
+    interval_hbm,
+    cell_row_hbm,
+    cell_col_hbm,
+    gain_hbm,
+    image_hbm,
+    turn_hbm,
+    twist_hbm,
+    resid_ref,
+    table,
+    turn_ref,
+    twist_ref,
     vis_ref,
     weight_ref,
     live_ref,
@@ -203,13 +218,6 @@
     cell_col_ref,
     gain_ref,
     image_ref,
-    first_hi_ref,
-    first_lo_ref,
-    last_hi_ref,
-    last_lo_ref,
-    twist_ref,
-    resid_ref,
-    dirty_ref,
     gain_all,
     part_out,
     part_in,
@@ -218,13 +226,14 @@
     lines,
     work_re,
     work_im,
-    table,
-    cells,
+    local_row,
+    local_col,
     values,
-    block_cos,
-    block_sin,
+    step_cos,
+    step_sin,
     fine_cos,
     fine_sin,
+    load_sem,
     gain_send,
     gain_recv,
     part_send,
@@ -237,6 +246,30 @@
     me = lax.axis_index("vis")
     facet = lax.axis_index("facet")
     side_x = image_ref.shape[0]
+    width = values.shape[2]
+    slots = vis_ref.shape[1]
+    part = slots // 2
+
+    order = (
+        (cell_row_hbm, cell_row_ref),
+        (cell_col_hbm, cell_col_ref),
+        (gain_hbm, gain_ref),
+        (image_hbm, image_ref),
+        (turn_hbm, turn_ref),
+        (twist_hbm, twist_ref),
+        (interval_hbm, interval_ref),
+        (station_p_hbm, station_p_ref),
+        (station_q_hbm, station_q_ref),
+        (live_hbm, live_ref),
+        (weight_hbm, weight_ref),
+        (vis_hbm, vis_ref),
+    )
+    loads = [
+        pltpu.make_async_copy(source, target, load_sem.at[place])
+        for place, (source, target) in enumerate(order)
+    ]
+    for load in loads:
+        load.start()
 
     def vis_peer(step):
         return lax.rem(me + step, n_vis)
@@ -275,6 +308,41 @@
         view = buffer.at[pl.ds(0, count)]
         pltpu.make_async_copy(view, view, sem).wait()
 
+    def pair_row(pair):
+        return lax.rem(pair, 4) * 4 + pair // 4
+
+    loads[0].wait()
+    loads[1].wait()
+
+    def order_cells(group, carry):
+        lanes = pl.ds(pl.multiple_of(group * 128, 128), 128)
+
+        def read(holder):
+            rows = pl.ds(holder * 4, 4)
+            return jnp.concatenate([cell_row_ref[rows, :], cell_col_ref[rows, :]], axis=0)
+
+        for turn, rows in enumerate(slots_to_pairs([read(4 * group + k) for k in range(4)])):
+            lane = lax.broadcasted_iota(jnp.int32, (4, 128), 1)
+            local_row[4 * turn : 4 * turn + 4, lanes] = rows[0:4] + ((lane >> 4) & 1) * 64
+            local_col[4 * turn : 4 * turn + 4, lanes] = rows[4:8]
+        return carry
+
+    lax.fori_loop(0, n_vis // 4, order_cells, 0)
+    cos, sin = unit_phase((local_col[...] * 8) & (SIDE - 1))
+    step_cos[...] = cos
+    step_sin[...] = sin
+
+    def fine_phases(pair, carry):
+        column = local_col[pl.ds(pair_row(pair), 1), :]
+        index = lax.broadcasted_iota(jnp.int32, (8, width), 0)
+        cos, sin = unit_phase((column * (me * side_x + index)) & (SIDE - 1))
+        fine_cos[pair] = cos
+        fine_sin[pair] = sin
+        return carry
+
+    lax.fori_loop(0, RADIX, fine_phases, 0)
+
+    loads[2].wait()
     intervals_here = gain_ref.shape[1]
     stations = gain_ref.shape[2]
     gain_all[me] = jnp.zeros((8, 256), F32)
@@ -285,13 +353,15 @@
     pl.semaphore_wait(barrier, n_vis + n_facet - 2)
     send_all(lambda peer: gain_all.at[me], gain_all, gain_send, gain_recv)
 
+    loads[3].wait()
     lines[...] = image_ref[...].T
+    loads[4].wait()
+    loads[5].wait()
+    first_hi = jnp.concatenate([turn_ref[:INNER], turn_ref[INNER : 2 * INNER]], axis=1)
+    first_lo = jnp.concatenate([turn_ref[2 * INNER : 3 * INNER], turn_ref[3 * INNER :]], axis=1)
     for b in range(RADIX):
-        part = lines[pl.ds(b, INNER, stride=RADIX), :].T
-        high, low = split_pair(part)
-        both = matmul(high, first_hi_ref[...]) + (
-            matmul(high, first_lo_ref[...]) + matmul(low, first_hi_ref[...])
-        )
+        high, low = split_pair(lines[pl.ds(b, INNER, stride=RADIX), :].T)
+        both = matmul(high, first_hi) + (matmul(high, first_lo) + matmul(low, first_hi))
         re, im = both[:, :INNER], both[:, INNER:]
         cos = twist_ref[0, b : b + 1, :]
         sin = twist_ref[1, b : b + 1, :]
@@ -309,88 +379,74 @@
 
     lax.fori_loop(0, side_x // 8, forward_rows, 0)
 
-    def order_cells(group, carry):
-        lanes = pl.ds(pl.multiple_of(group * 128, 128), 128)
-
-        def read(holder):
-            rows = pl.ds(holder * 4, 4)
-            return jnp.concatenate([cell_row_ref[rows, :], cell_col_ref[rows, :]], axis=0)
-
-        for turn, rows in enumerate(slots_to_pairs(read, group)):
-            cells[8 * turn : 8 * turn + 8, lanes] = rows
-        return carry
-
-    lax.fori_loop(0, n_vis // 4, order_cells, 0)
-
-    width = cells.shape[1]
     chunk_w = 256
-
-    def pair_row(pair):
-        return lax.rem(pair, 4) * 8 + pair // 4
+    blocks_x = side_x // 8
 
     def one_hot(pair, lanes):
-        local = cells[pl.ds(pair_row(pair), 1), lanes]
-        lane = lax.broadcasted_iota(jnp.int32, local.shape, 1)
-        local = local + ((lane >> 4) & 1) * 64
+        local = local_row[pl.ds(pair_row(pair), 1), lanes]
         index = lax.broadcasted_iota(jnp.int32, (INNER, local.shape[1]), 0)
         return jnp.where(index == local, 1.0, 0.0).astype(BF16)
 
+    def value_row(pair):
+        return lax.rem(pair, 4) * 4 + lax.rem(pair // 4, 2)
+
     def forward_pair(pair, carry):
-        column = cells[pl.ds(pair_row(pair) + 4, 1), :]
-        index = lax.broadcasted_iota(jnp.int32, (8, width), 0)
-        cos, sin = unit_phase((column * (me * side_x + 8 * index)) & (SIDE - 1))
-        block_cos[pair] = cos
-        block_sin[pair] = sin
-        cos, sin = unit_phase((column * index) & (SIDE - 1))
-        fine_cos[pair] = cos
-        fine_sin[pair] = sin
         high, low = split_pair(table[pair])
         both = jnp.concatenate([high, low], axis=0)
+        half = pair // 8
         for start in range(0, width, chunk_w):
             lanes = slice(start, start + chunk_w)
             picked = matmul(both, one_hot(pair, lanes))
             picked = picked[: 2 * side_x] + picked[2 * side_x :]
-            sum_re = 0.0
-            sum_im = 0.0
-            for block in range(side_x // 8):
+            cos = step_cos[pl.ds(pair_row(pair), 1), lanes]
+            sin = step_sin[pl.ds(pair_row(pair), 1), lanes]
+            last = 8 * (blocks_x - 1)
+            sum_re = picked[last : last + 8]
+            sum_im = picked[side_x + last : side_x + last + 8]
+            for block in range(blocks_x - 2, -1, -1):
                 re = picked[8 * block : 8 * block + 8]
                 im = picked[side_x + 8 * block : side_x + 8 * block + 8]
-                cos = block_cos[pair, block : block + 1, lanes]
-                sin = block_sin[pair, block : block + 1, lanes]
-                sum_re = sum_re + (re * cos + im * sin)
-                sum_im = sum_im + (im * cos - re * sin)
+                sum_re, sum_im = (
+                    re + (sum_re * cos + sum_im * sin),
+                    im + (sum_im * cos - sum_re * sin),
+                )
             cos = fine_cos[pair, :, lanes]
             sin = fine_sin[pair, :, lanes]
             out_re = jnp.sum(sum_re * cos + sum_im * sin, axis=0, keepdims=True)
             out_im = jnp.sum(sum_im * cos - sum_re * sin, axis=0, keepdims=True)
-            values[pl.ds(pair_row(pair), 1), lanes] = out_re
-            values[pl.ds(pair_row(pair) + 4, 1), lanes] = out_im
+            values[half, pl.ds(value_row(pair), 1), lanes] = out_re
+            values[half, pl.ds(value_row(pair) + 2, 1), lanes] = out_im
         return carry
 
-    lax.fori_loop(0, RADIX, forward_pair, 0)
-
-    def pack_values(group, carry):
-        lanes = pl.ds(pl.multiple_of(group * 128, 128), 128)
-        rows = [values[8 * turn : 8 * turn + 8, lanes] for turn in range(4)]
-        for member, block in enumerate(pairs_to_slots(rows)):
-            part_out[4 * group + member] = block
-        return carry
-
-    lax.fori_loop(0, n_vis // 4, pack_values, 0)
-    send_all(lambda peer: part_out.at[peer], part_in, part_send, part_recv)
-    part_in[me] = part_out[me]
-
+    for half in range(2):
+        lax.fori_loop(8 * half, 8 * half + 8, forward_pair, 0)
+
+        def pack_values(group, carry):
+            lanes = pl.ds(pl.multiple_of(group * 128, 128), 128)
+            rows = [values[half, 4 * turn : 4 * turn + 4, lanes] for turn in range(4)]
+            for member, block in enumerate(pairs_to_slots(rows)):
+                part_out[half, 4 * group + member] = block
+            return carry
+
+        lax.fori_loop(0, n_vis // 4, pack_values, 0)
+        send_all(
+            lambda peer: part_out.at[half, peer],
+            part_in.at[half],
+            part_send.at[half],
+            part_recv.at[half],
+        )
+        part_in[half, me] = part_out[half, me]
+
+    for load in loads[6:]:
+        load.wait()
     wait_blocks(gain_all, n_vis - 1, gain_recv)
     high, low = split_pair(gain_all[...].reshape(n_vis * 8, 256).T)
     both = jnp.concatenate([high, low], axis=0)
     interval = wide_row(interval_ref[...])
     gain_row = (interval >> 2) * 8 + (interval & 3)
-    station_p = wide_row(station_p_ref[...])
-    station_q = wide_row(station_q_ref[...])
-    slots = interval.shape[1]
     station = lax.broadcasted_iota(jnp.int32, (64, slots), 0)
-    at_p = jnp.where(station == station_p, 1.0, 0.0)
-    at_q = jnp.where(station == station_q, 1.0, 0.0)
+    at_p = jnp.where(station == wide_row(station_p_ref[...]), 1.0, 0.0)
+    at_q = jnp.where(station == wide_row(station_q_ref[...]), 1.0, 0.0)
     index = lax.broadcasted_iota(jnp.int32, (n_vis * 8, slots), 0)
     jones_p = []
     jones_q = []
@@ -406,62 +462,68 @@
     live = wide_row(live_ref[...]).astype(F32)
     scale = wide_row(weight_ref[...]) * live
 
-    wait_blocks(part_in, n_vis - 1, part_recv)
-    model = jnp.sum(part_in[...], axis=0) * (1.0 / SIDE)
-    model_re = wide_row(model[0:4])
-    model_im = wide_row(model[4:8])
-    pred_in[facet, 0:4, :] = model_re * outer_re - model_im * outer_im
-    pred_in[facet, 4:8, :] = model_re * outer_im + model_im * outer_re
-
-    def send_pred(step, carry):
-        pltpu.make_async_remote_copy(
-            src_ref=pred_in.at[facet],
-            dst_ref=pred_in.at[facet],
-            send_sem=pred_send,
-            recv_sem=pred_recv,
-            device_id=(me, facet_peer(step)),
-            device_id_type=MESH,
-        ).start()
-        return carry
-
-    lax.fori_loop(1, n_facet, send_pred, 0)
-    wait_blocks(pred_in, n_facet - 1, pred_recv)
-    predicted = pred_in[0]
-    for other in range(1, n_facet):
-        predicted = predicted + pred_in[other]
-    resid = (vis_ref[...] - predicted) * live
-    resid_ref[...] = resid
-    stokes_re, stokes_im = jones_stokes(jones_p, jones_q, [resid[c : c + 1] for c in range(8)])
-    stokes_in[me, 0:4, :] = tall_block(stokes_re * scale)
-    stokes_in[me, 4:8, :] = tall_block(stokes_im * scale)
-    send_all(lambda peer: stokes_in.at[me], stokes_in, stokes_send, stokes_recv)
-    wait_blocks(stokes_in, n_vis - 1, stokes_recv)
-
-    def order_stokes(group, carry):
-        lanes = pl.ds(pl.multiple_of(group * 128, 128), 128)
-        for turn, rows in enumerate(slots_to_pairs(lambda holder: stokes_in[holder], group)):
-            values[8 * turn : 8 * turn + 8, lanes] = rows
-        return carry
-
-    lax.fori_loop(0, n_vis // 4, order_stokes, 0)
+    for half in range(2):
+        here = slice(half * part, (half + 1) * part)
+        wait_blocks(part_in.at[half], n_vis - 1, part_recv.at[half])
+        model = jnp.sum(part_in[half], axis=0) * (1.0 / SIDE)
+        model_re = wide_row(model[0:2])
+        model_im = wide_row(model[2:4])
+        own_re, own_im = outer_re[:, here], outer_im[:, here]
+        pred_in[half, facet, 0:4, :] = model_re * own_re - model_im * own_im
+        pred_in[half, facet, 4:8, :] = model_re * own_im + model_im * own_re
+
+        def send_pred(step, carry):
+            pltpu.make_async_remote_copy(
+                src_ref=pred_in.at[half, facet],
+                dst_ref=pred_in.at[half, facet],
+                send_sem=pred_send.at[half],
+                recv_sem=pred_recv.at[half],
+                device_id=(me, facet_peer(step)),
+                device_id_type=MESH,
+            ).start()
+            return carry
+
+        lax.fori_loop(1, n_facet, send_pred, 0)
+
+    for half in range(2):
+        here = slice(half * part, (half + 1) * part)
+        wait_blocks(pred_in.at[half], n_facet - 1, pred_recv.at[half])
+        predicted = pred_in[half, 0]
+        for other in range(1, n_facet):
+            predicted = predicted + pred_in[half, other]
+        resid = (vis_ref[:, here] - predicted) * live[:, here]
+        resid_ref[:, here] = resid
+        stokes_re, stokes_im = jones_stokes(
+            [gain[:, here] for gain in jones_p],
+            [gain[:, here] for gain in jones_q],
+            [resid[comp : comp + 1] for comp in range(8)],
+        )
+        stokes_in[half, me, 0:2, :] = tall_block(stokes_re * scale[:, here])
+        stokes_in[half, me, 2:4, :] = tall_block(stokes_im * scale[:, here])
+        send_all(
+            lambda peer: stokes_in.at[half, me],
+            stokes_in.at[half],
+            stokes_send.at[half],
+            stokes_recv.at[half],
+        )
 
     def backward_pair(pair, carry):
         total = jnp.zeros((4 * side_x, INNER), F32)
+        half = pair // 8
         for start in range(0, width, chunk_w):
             lanes = slice(start, start + chunk_w)
-            re = values[pl.ds(pair_row(pair), 1), lanes]
-            im = values[pl.ds(pair_row(pair) + 4, 1), lanes]
+            re = values[half, pl.ds(value_row(pair), 1), lanes]
+            im = values[half, pl.ds(value_row(pair) + 2, 1), lanes]
             cos = fine_cos[pair, :, lanes]
             sin = fine_sin[pair, :, lanes]
-            fine_re = re * cos - im * sin
-            fine_im = re * sin + im * cos
-            real_rows = []
-            imag_rows = []
-            for block in range(side_x // 8):
-                cos = block_cos[pair, block : block + 1, lanes]
-                sin = block_sin[pair, block : block + 1, lanes]
-                real_rows.append(fine_re * cos - fine_im * sin)
-                imag_rows.append(fine_re * sin + fine_im * cos)
+            real_rows = [re * cos - im * sin]
+            imag_rows = [re * sin + im * cos]
+            cos = step_cos[pl.ds(pair_row(pair), 1), lanes]
+            sin = step_sin[pl.ds(pair_row(pair), 1), lanes]
+            for _ in range(blocks_x - 1):
+                re, im = real_rows[-1], imag_rows[-1]
+                real_rows.append(re * cos - im * sin)
+                imag_rows.append(re * sin + im * cos)
             high, low = split_pair(jnp.concatenate(real_rows + imag_rows, axis=0))
             both = jnp.concatenate([high, low], axis=0)
             total = total + lax.dot_general(
@@ -473,7 +535,44 @@
         table[pair] = total[: 2 * side_x] + total[2 * side_x :]
         return carry
 
-    lax.fori_loop(0, RADIX, backward_pair, 0)
+    for half in range(2):
+        wait_blocks(stokes_in.at[half], n_vis - 1, stokes_recv.at[half])
+
+        def order_stokes(group, carry):
+            lanes = pl.ds(pl.multiple_of(group * 128, 128), 128)
+            blocks = [stokes_in[half, 4 * group + member] for member in range(4)]
+            for turn, rows in enumerate(slots_to_pairs(blocks)):
+                values[half, 4 * turn : 4 * turn + 4, lanes] = rows
+            return carry
+
+        lax.fori_loop(0, n_vis // 4, order_stokes, 0)
+        lax.fori_loop(8 * half, 8 * half + 8, backward_pair, 0)
+
+    wait_blocks(gain_all, n_vis - 1, gain_send)
+    for half in range(2):
+        wait_blocks(part_in.at[half], n_vis - 1, part_send.at[half])
+        wait_blocks(pred_in.at[half], n_facet - 1, pred_send.at[half])
+        wait_blocks(stokes_in.at[half], n_vis - 1, stokes_send.at[half])
+
+
+def image_kernel(
+    factor,
+    resid_ref,
+    table,
+    turn_ref,
+    twist_ref,
+    resid_hbm,
+    dirty_hbm,
+    work_re,
+    work_im,
+    lines,
+    dirty,
+    resid_sem,
+    dirty_sem,
+):
+    side_x = dirty.shape[0]
+    keep = pltpu.make_async_copy(resid_ref, resid_hbm, resid_sem)
+    keep.start()
 
     def backward_rows(chunk, carry):
         rows = pl.ds(pl.multiple_of(chunk * 8, 8), 8)
@@ -489,19 +588,25 @@
 
     lax.fori_loop(0, side_x // 8, backward_rows, 0)
 
-    factor = 4.0 / math.sqrt(slots * n_vis)
+    last_hi = turn_ref[: 2 * INNER]
+    last_lo = turn_ref[2 * INNER :]
     for b in range(RADIX):
         high, low = split_pair(jnp.concatenate([work_re[b], work_im[b]], axis=1))
-        part = matmul(high, last_hi_ref[...]) + (
-            matmul(high, last_lo_ref[...]) + matmul(low, last_hi_ref[...])
+        part = matmul(high, last_hi) + (matmul(high, last_lo) + matmul(low, last_hi))
+        lines[pl.ds(b, INNER, stride=RADIX), :] = (part * factor).T
+    count = dirty_sem.shape[0]
+    wide = SIDE // count
+    copies = []
+    for piece in range(count):
+        here = slice(piece * wide, (piece + 1) * wide)
+        dirty[:, here] = lines[here, :].T
+        copies.append(
+            pltpu.make_async_copy(dirty.at[:, here], dirty_hbm.at[:, here], dirty_sem.at[piece])
         )
-        lines[pl.ds(b, INNER, stride=RADIX), :] = (part * factor).T
-    dirty_ref[...] = lines[...].T
-
-    wait_blocks(gain_all, n_vis - 1, gain_send)
-    wait_blocks(part_in, n_vis - 1, part_send)
-    wait_blocks(pred_in, n_facet - 1, pred_send)
-    wait_blocks(stokes_in, n_vis - 1, stokes_send)
+        copies[-1].start()
+    for copy in copies:
+        copy.wait()
+    keep.wait()
 
 
 def per_device(
@@ -525,38 +630,8 @@
     def rows_of(array):
         return array.reshape(-1, 128)
 
-    tables = [jnp.asarray(table) for table in make_tables()]
-    vmem = pl.BlockSpec(memory_space=pltpu.VMEM)
-    resid, dirty = pl.pallas_call(
-        functools.partial(kernel, n_vis, n_facet),
-        out_shape=(
-            jax.ShapeDtypeStruct((8, slots), F32),
-            jax.ShapeDtypeStruct((side_x, SIDE), F32),
-        ),
-        in_specs=[vmem] * 15,
-        out_specs=(vmem, vmem),
-        scratch_shapes=[
-            pltpu.VMEM((n_vis, 8, 256), F32),
-            pltpu.VMEM((n_vis, 8, 128), F32),
-            pltpu.VMEM((n_vis, 8, 128), F32),
-            pltpu.VMEM((n_facet, 8, slots), F32),
-            pltpu.VMEM((n_vis, 8, 128), F32),
-            pltpu.VMEM((SIDE, side_x), F32),
-            pltpu.VMEM((RADIX, side_x, INNER), F32),
-            pltpu.VMEM((RADIX, side_x, INNER), F32),
-            pltpu.VMEM((RADIX, 2 * side_x, INNER), F32),
-            pltpu.VMEM((32, width), jnp.int32),
-            pltpu.VMEM((32, width), F32),
-            pltpu.VMEM((RADIX, 8, width), F32),
-            pltpu.VMEM((RADIX, 8, width), F32),
-            pltpu.VMEM((RADIX, 8, width), F32),
-            pltpu.VMEM((RADIX, 8, width), F32),
-        ]
-        + [pltpu.SemaphoreType.DMA(())] * 8,
-        compiler_params=pltpu.CompilerParams(
-            collective_id=0, has_side_effects=True, vmem_limit_bytes=40 * 1024 * 1024
-        ),
-    )(
+    turn, twist = [jnp.asarray(table) for table in make_tables()]
+    given = [
         visibilities,
         rows_of(weights),
         rows_of(live_slots),
@@ -567,8 +642,66 @@
         rows_of(cell_col),
         jones_gains[0],
         model_image[0],
-        *tables,
-    )
+        turn,
+        twist,
+    ]
+    in_hbm = pl.BlockSpec(memory_space=pltpu.HBM)
+    in_vmem = pl.BlockSpec(memory_space=pltpu.VMEM)
+    work = pltpu.VMEM((RADIX, side_x, INNER), F32)
+    kept = pl.pallas_call(
+        functools.partial(exchange_kernel, n_vis, n_facet),
+        out_shape=(
+            pltpu.VMEM((8, slots), F32),
+            pltpu.VMEM((RADIX, 2 * side_x, INNER), F32),
+            pltpu.VMEM(turn.shape, turn.dtype),
+            pltpu.VMEM(twist.shape, twist.dtype),
+        ),
+        in_specs=[in_hbm] * len(given),
+        out_specs=(in_vmem,) * 4,
+        scratch_shapes=[pltpu.VMEM(array.shape, array.dtype) for array in given[:-2]]
+        + [
+            pltpu.VMEM((n_vis, 8, 256), F32),
+            pltpu.VMEM((2, n_vis, 4, 128), F32),
+            pltpu.VMEM((2, n_vis, 4, 128), F32),
+            pltpu.VMEM((2, n_facet, 8, slots // 2), F32),
+            pltpu.VMEM((2, n_vis, 4, 128), F32),
+            pltpu.VMEM((SIDE, side_x), F32),
+            work,
+            work,
+            pltpu.VMEM((16, width), jnp.int32),
+            pltpu.VMEM((16, width), jnp.int32),
+            pltpu.VMEM((2, 16, width), F32),
+            pltpu.VMEM((16, width), F32),
+            pltpu.VMEM((16, width), F32),
+            pltpu.VMEM((RADIX, 8, width), F32),
+            pltpu.VMEM((RADIX, 8, width), F32),
+            pltpu.SemaphoreType.DMA((len(given),)),
+            pltpu.SemaphoreType.DMA(()),
+            pltpu.SemaphoreType.DMA(()),
+        ]
+        + [pltpu.SemaphoreType.DMA((2,))] * 6,
+        compiler_params=pltpu.CompilerParams(
+            collective_id=0, has_side_effects=True, vmem_limit_bytes=40 * 1024 * 1024
+        ),
+    )(*[pltpu.with_memory_space_constraint(array, pltpu.HBM) for array in given])
+    resid, dirty = pl.pallas_call(
+        functools.partial(image_kernel, 4.0 / math.sqrt(slots * n_vis)),
+        out_shape=(
+            pltpu.HBM((8, slots), F32),
+            pltpu.HBM((side_x, SIDE), F32),
+        ),
+        in_specs=[in_vmem] * 4,
+        out_specs=(in_hbm, in_hbm),
+        scratch_shapes=[
+            work,
+            work,
+            pltpu.VMEM((SIDE, side_x), F32),
+            pltpu.VMEM((side_x, SIDE), F32),
+            pltpu.SemaphoreType.DMA(()),
+            pltpu.SemaphoreType.DMA((4,)),
+        ],
+        compiler_params=pltpu.CompilerParams(vmem_limit_bytes=40 * 1024 * 1024),
+    )(*kept)
     return resid, dirty[None]
 
 

time: 60.9 us -> 44.6 us (0.73)
  local copies, waits for them, and re-layouts: 13 us -> 0 us
  Pallas kernels: 46.5 us -> 43.8 us
    unnamed x32 -> x0, local copies, waits for them, and re-layouts: 13 us -> none
    pallas_call x1 -> x2, Pallas kernels: 46.5 us -> 43.8 us  [the longest x1 41.7 us: per_device(): pl.pallas_call(functools.partial(exchange_kernel, n_vis, n_facet), out_sh...]
where the time goes in v1:
time: 44.6 us; the launch traced here: 44.5 us
  Pallas kernels  43.8 us (98%)
  between operations  0.64 us (1%)
    pallas_call x1, Pallas kernels, per_device(): pl.pallas_call(functools.partial(exchange_kernel, n_vis, n_facet), out_sh...  41.7 us
    pallas_call x1, Pallas kernels, per_device(): pl.pallas_call(functools.partial(image_kernel, 4.0 / math.sqrt(slots * n_...  2.16 us

profile of v1, /device:TPU:1, one launch (start us, length us, event | category | flops | bytes accessed | tf_op | source)
XLA Modules:
  0.0 44.5 jit_solution(3746462121519238850)
XLA Ops:
  0.6 41.7 %shard_map.131 = (f32[8,512]{1,0:T(8,128)S(1)}, f32[16,128,128]{2,1,0:T(8,128)S(1)}, bf16[512,128]{1,0:T(8,128)(2,1)S(1)}, f32[2,16,128]{2,1,0:T(8,128)S(1)}) custom-call(f32[8,512]{1,0:T(8,128)} %vis_hbm.1, f32[4,128]{1,0:T(4,128)} %bitcast.14, s32[4,128]{1,0:T(4,128)} %bitcast.15, s32[4,128]{1,0:T(4,128)} %bitcast.16, s32[4,128]{1,0:T(4,128)} %bitcast.17, ...), custom_call_target="tpu_custom_call" | custom-call | tf_op jit(solution)/shard_map/pallas_call | solution.py:651
  42.3 2.2 %shard_map.132 = (f32[8,512]{1,0:T(8,128)}, f32[64,2048]{1,0:T(8,128)}) custom-call(f32[8,512]{1,0:T(8,128)S(1)} %get-tuple-element.8.resid_ref, f32[16,128,128]{2,1,0:T(8,128)S(1)} %get-tuple-element.9.table, bf16[512,128]{1,0:T(8,128)(2,1)S(1)} %get-tuple-element.10.turn_ref, f32[2,16,128]{2,1,0:T(8,128)S(1)} %get-tuple-element.11.twist_ref), custom_call_target="tpu_custom_call" | custom-call | tf_op jit(solution)/shard_map/pallas_call | solution.py:687

commit v2 on v1

--- a/solution.py
+++ b/solution.py
@@ -110,6 +110,23 @@
     cos_val = jnp.where(((quarter + 1) & 2) == 2, -cos_mag, cos_mag)
     sin_val = jnp.where((quarter & 2) == 2, -sin_mag, sin_mag)
     return cos_val, sin_val
+
+
+def pick_lanes(value, index):
+    numbers = lax.GatherDimensionNumbers(
+        offset_dims=(),
+        collapsed_slice_dims=(1,),
+        start_index_map=(1,),
+        operand_batching_dims=(0,),
+        start_indices_batching_dims=(0,),
+    )
+    return lax.gather(
+        value,
+        index[..., None],
+        numbers,
+        slice_sizes=(1, 1),
+        mode=lax.GatherScatterMode.PROMISE_IN_BOUNDS,
+    )
 
 
 def lane_block(shape):
@@ -246,7 +263,7 @@
     me = lax.axis_index("vis")
     facet = lax.axis_index("facet")
     side_x = image_ref.shape[0]
-    width = values.shape[2]
+    width = values.shape[3]
     slots = vis_ref.shape[1]
     part = slots // 2
 
@@ -271,38 +288,45 @@
     for load in loads:
         load.start()
 
+    ring_z, ring_y = n_vis // 4, n_facet // 2
+    side = me // (2 * ring_z)
+    vis_steps = [
+        (away, along, core)
+        for away in range(2)
+        for along in range(ring_z)
+        for core in range(2)
+        if (away, along, core) != (0, 0, 0)
+    ]
+    vis_steps.sort(key=lambda step: (-2 * step[0] - min(step[1], ring_z - step[1]), -step[2]))
+    facet_steps = [(along, away) for along in range(ring_y) for away in range(2) if along or away]
+    facet_steps.sort(key=lambda step: -min(step[0], ring_y - step[0]) - step[1])
+
     def vis_peer(step):
-        return lax.rem(me + step, n_vis)
+        away, along, core = step
+        z = lax.rem(me // 2 + along, ring_z)
+        return ((side ^ away) * ring_z + z) * 2 + ((me & 1) ^ core)
 
     def facet_peer(step):
-        return lax.rem(facet + step, n_facet)
+        along, away = step
+        return lax.rem(facet // 2 + along, ring_y) * 2 + ((facet & 1) ^ away)
 
     barrier = pltpu.get_barrier_semaphore()
-
-    def greet_vis(step, carry):
+    for step in vis_steps:
         pl.semaphore_signal(barrier, 1, device_id=(vis_peer(step), facet), device_id_type=MESH)
-        return carry
-
-    def greet_facet(step, carry):
+    for step in facet_steps:
         pl.semaphore_signal(barrier, 1, device_id=(me, facet_peer(step)), device_id_type=MESH)
-        return carry
-
-    lax.fori_loop(1, n_vis, greet_vis, 0)
-    lax.fori_loop(1, n_facet, greet_facet, 0)
 
     def send_all(source, target, send_sem, recv_sem):
-        def send(step, carry):
+        for step in vis_steps:
+            peer = vis_peer(step)
             pltpu.make_async_remote_copy(
-                src_ref=source(vis_peer(step)),
+                src_ref=source(peer),
                 dst_ref=target.at[me],
                 send_sem=send_sem,
-                recv_sem=recv_sem,
-                device_id=(vis_peer(step), facet),
+                recv_sem=recv_sem(step),
+                device_id=(peer, facet),
                 device_id_type=MESH,
             ).start()
-            return carry
-
-        lax.fori_loop(1, n_vis, send, 0)
 
     def wait_blocks(buffer, count, sem):
         view = buffer.at[pl.ds(0, count)]
@@ -314,8 +338,11 @@
     loads[0].wait()
     loads[1].wait()
 
+    def group_place(group):
+        return group // 4, pl.ds(pl.multiple_of(lax.rem(group, 4) * 128, 128), 128)
+
     def order_cells(group, carry):
-        lanes = pl.ds(pl.multiple_of(group * 128, 128), 128)
+        place, lanes = group_place(group)
 
         def read(holder):
             rows = pl.ds(holder * 4, 4)
@@ -323,24 +350,15 @@
 
         for turn, rows in enumerate(slots_to_pairs([read(4 * group + k) for k in range(4)])):
             lane = lax.broadcasted_iota(jnp.int32, (4, 128), 1)
-            local_row[4 * turn : 4 * turn + 4, lanes] = rows[0:4] + ((lane >> 4) & 1) * 64
-            local_col[4 * turn : 4 * turn + 4, lanes] = rows[4:8]
+            local_row[place, 4 * turn : 4 * turn + 4, lanes] = rows[0:4] + ((lane >> 4) & 1) * 64
+            local_col[place, 4 * turn : 4 * turn + 4, lanes] = rows[4:8]
         return carry
 
-    lax.fori_loop(0, n_vis // 4, order_cells, 0)
-    cos, sin = unit_phase((local_col[...] * 8) & (SIDE - 1))
-    step_cos[...] = cos
-    step_sin[...] = sin
-
-    def fine_phases(pair, carry):
-        column = local_col[pl.ds(pair_row(pair), 1), :]
-        index = lax.broadcasted_iota(jnp.int32, (8, width), 0)
-        cos, sin = unit_phase((column * (me * side_x + index)) & (SIDE - 1))
-        fine_cos[pair] = cos
-        fine_sin[pair] = sin
-        return carry
-
-    lax.fori_loop(0, RADIX, fine_phases, 0)
+    lax.fori_loop(0, n_vis // 4, order_cells, 0, unroll=4)
+    for place in range(2):
+        cos, sin = unit_phase((local_col[place] * 8) & (SIDE - 1))
+        step_cos[place] = cos
+        step_sin[place] = sin
 
     loads[2].wait()
     intervals_here = gain_ref.shape[1]
@@ -351,7 +369,7 @@
         gain_all[me, 4 * half : 4 * half + intervals_here, lane : lane + stations] = gain_ref[comp]
 
     pl.semaphore_wait(barrier, n_vis + n_facet - 2)
-    send_all(lambda peer: gain_all.at[me], gain_all, gain_send, gain_recv)
+    send_all(lambda peer: gain_all.at[me], gain_all, gain_send, lambda step: gain_recv)
 
     loads[3].wait()
     lines[...] = image_ref[...].T
@@ -359,14 +377,24 @@
     loads[5].wait()
     first_hi = jnp.concatenate([turn_ref[:INNER], turn_ref[INNER : 2 * INNER]], axis=1)
     first_lo = jnp.concatenate([turn_ref[2 * INNER : 3 * INNER], turn_ref[3 * INNER :]], axis=1)
-    for b in range(RADIX):
-        high, low = split_pair(lines[pl.ds(b, INNER, stride=RADIX), :].T)
-        both = matmul(high, first_hi) + (matmul(high, first_lo) + matmul(low, first_hi))
-        re, im = both[:, :INNER], both[:, INNER:]
-        cos = twist_ref[0, b : b + 1, :]
-        sin = twist_ref[1, b : b + 1, :]
-        work_re[b] = re * cos + im * sin
-        work_im[b] = im * cos - re * sin
+    first_twice = jnp.concatenate([first_hi, first_hi], axis=0)
+    group_b = 8
+    for start in range(0, RADIX, group_b):
+        halves = [
+            split_pair(lines[pl.ds(b, INNER, stride=RADIX), :].T)
+            for b in range(start, start + group_b)
+        ]
+        high = jnp.concatenate([pair[0] for pair in halves], axis=0)
+        low = jnp.concatenate([pair[1] for pair in halves], axis=0)
+        both = matmul(jnp.concatenate([high, low], axis=1), first_twice) + matmul(high, first_lo)
+        for place in range(group_b):
+            b = start + place
+            here = both[place * side_x : (place + 1) * side_x]
+            re, im = here[:, :INNER], here[:, INNER:]
+            cos = twist_ref[0, b : b + 1, :]
+            sin = twist_ref[1, b : b + 1, :]
+            work_re[b] = re * cos + im * sin
+            work_im[b] = im * cos - re * sin
 
     def forward_rows(chunk, carry):
         rows = pl.ds(pl.multiple_of(chunk * 8, 8), 8)
@@ -377,13 +405,13 @@
             table[q, rows_im, :] = vals[q][1]
         return carry
 
-    lax.fori_loop(0, side_x // 8, forward_rows, 0)
+    lax.fori_loop(0, side_x // 8, forward_rows, 0, unroll=4)
 
     chunk_w = 256
+    by_lanes = 256
     blocks_x = side_x // 8
 
-    def one_hot(pair, lanes):
-        local = local_row[pl.ds(pair_row(pair), 1), lanes]
+    def hot_columns(local):
         index = lax.broadcasted_iota(jnp.int32, (INNER, local.shape[1]), 0)
         return jnp.where(index == local, 1.0, 0.0).astype(BF16)
 
@@ -391,49 +419,73 @@
         return lax.rem(pair, 4) * 4 + lax.rem(pair // 4, 2)
 
     def forward_pair(pair, carry):
+        half = pair // 8
+        row = pl.ds(pair_row(pair), 1)
         high, low = split_pair(table[pair])
         both = jnp.concatenate([high, low], axis=0)
-        half = pair // 8
-        for start in range(0, width, chunk_w):
-            lanes = slice(start, start + chunk_w)
-            picked = matmul(both, one_hot(pair, lanes))
+
+        def picked_by_matmul(local):
+            picked = matmul(both, hot_columns(local))
             picked = picked[: 2 * side_x] + picked[2 * side_x :]
-            cos = step_cos[pl.ds(pair_row(pair), 1), lanes]
-            sin = step_sin[pl.ds(pair_row(pair), 1), lanes]
-            last = 8 * (blocks_x - 1)
-            sum_re = picked[last : last + 8]
-            sum_im = picked[side_x + last : side_x + last + 8]
-            for block in range(blocks_x - 2, -1, -1):
-                re = picked[8 * block : 8 * block + 8]
-                im = picked[side_x + 8 * block : side_x + 8 * block + 8]
-                sum_re, sum_im = (
-                    re + (sum_re * cos + sum_im * sin),
-                    im + (sum_im * cos - sum_re * sin),
-                )
-            cos = fine_cos[pair, :, lanes]
-            sin = fine_sin[pair, :, lanes]
-            out_re = jnp.sum(sum_re * cos + sum_im * sin, axis=0, keepdims=True)
-            out_im = jnp.sum(sum_im * cos - sum_re * sin, axis=0, keepdims=True)
-            values[half, pl.ds(value_row(pair), 1), lanes] = out_re
-            values[half, pl.ds(value_row(pair) + 2, 1), lanes] = out_im
+            return lambda first: picked[first : first + 8]
+
+        def picked_by_lanes(local):
+            index = jnp.broadcast_to(local, (8, INNER))
+            return lambda first: pick_lanes(table[pair, first : first + 8, :], index)
+
+        pieces = [(start, INNER, picked_by_lanes) for start in range(0, by_lanes, INNER)]
+        pieces += [(start, 256, picked_by_matmul) for start in range(by_lanes, width, 256)]
+        for place in range(2):
+            out_re = []
+            out_im = []
+            whole_index = local_row[place, row, :]
+            whole_column = local_col[place, row, :]
+            whole_cos = step_cos[place, row, :]
+            whole_sin = step_sin[place, row, :]
+            x_index = me * side_x + lax.broadcasted_iota(jnp.int32, (8, width), 0)
+            all_cos, all_sin = unit_phase((whole_column * x_index) & (SIDE - 1))
+            fine_cos[pair, place] = all_cos
+            fine_sin[pair, place] = all_sin
+            for start, size, picker in pieces:
+                lanes = slice(start, start + size)
+                pick = picker(whole_index[:, lanes])
+                cos = jnp.broadcast_to(whole_cos[:, lanes], (8, size))
+                sin = jnp.broadcast_to(whole_sin[:, lanes], (8, size))
+                sum_re = pick(8 * blocks_x - 8)
+                sum_im = pick(side_x + 8 * blocks_x - 8)
+                for block in range(blocks_x - 2, -1, -1):
+                    re = pick(8 * block)
+                    im = pick(side_x + 8 * block)
+                    sum_re, sum_im = (
+                        re + (sum_re * cos + sum_im * sin),
+                        im + (sum_im * cos - sum_re * sin),
+                    )
+                cos = all_cos[:, lanes]
+                sin = all_sin[:, lanes]
+                out_re.append(jnp.sum(sum_re * cos + sum_im * sin, axis=0, keepdims=True))
+                out_im.append(jnp.sum(sum_im * cos - sum_re * sin, axis=0, keepdims=True))
+            re_row = pl.ds(value_row(pair), 1)
+            im_row = pl.ds(value_row(pair) + 2, 1)
+            values[half, place, re_row, :] = jnp.concatenate(out_re, axis=1)
+            values[half, place, im_row, :] = jnp.concatenate(out_im, axis=1)
         return carry
 
     for half in range(2):
-        lax.fori_loop(8 * half, 8 * half + 8, forward_pair, 0)
+        lax.fori_loop(8 * half, 8 * half + 8, forward_pair, 0, unroll=4)
 
         def pack_values(group, carry):
-            lanes = pl.ds(pl.multiple_of(group * 128, 128), 128)
-            rows = [values[half, 4 * turn : 4 * turn + 4, lanes] for turn in range(4)]
+            place, lanes = group_place(group)
+            rows = [values[half, place, 4 * turn : 4 * turn + 4, lanes] for turn in range(4)]
             for member, block in enumerate(pairs_to_slots(rows)):
                 part_out[half, 4 * group + member] = block
             return carry
 
-        lax.fori_loop(0, n_vis // 4, pack_values, 0)
+        lax.fori_loop(0, n_vis // 4, pack_values, 0, unroll=8)
         send_all(
             lambda peer: part_out.at[half, peer],
             part_in.at[half],
             part_send.at[half],
-            part_recv.at[half],
+            lambda step: part_recv.at[half],
         )
         part_in[half, me] = part_out[half, me]
 
@@ -472,7 +524,7 @@
         pred_in[half, facet, 0:4, :] = model_re * own_re - model_im * own_im
         pred_in[half, facet, 4:8, :] = model_re * own_im + model_im * own_re
 
-        def send_pred(step, carry):
+        for step in facet_steps:
             pltpu.make_async_remote_copy(
                 src_ref=pred_in.at[half, facet],
                 dst_ref=pred_in.at[half, facet],
@@ -481,9 +533,6 @@
                 device_id=(me, facet_peer(step)),
                 device_id_type=MESH,
             ).start()
-            return carry
-
-        lax.fori_loop(1, n_facet, send_pred, 0)
 
     for half in range(2):
         here = slice(half * part, (half + 1) * part)
@@ -504,22 +553,28 @@
             lambda peer: stokes_in.at[half, me],
             stokes_in.at[half],
             stokes_send.at[half],
-            stokes_recv.at[half],
+            lambda step: stokes_recv.at[half, step[0]],
         )
 
-    def backward_pair(pair, carry):
+    def backward_pair(pair, place, first):
         total = jnp.zeros((4 * side_x, INNER), F32)
         half = pair // 8
+        row = pl.ds(pair_row(pair), 1)
+        whole_re = values[half, place, pl.ds(value_row(pair), 1), :]
+        whole_im = values[half, place, pl.ds(value_row(pair) + 2, 1), :]
+        whole_index = local_row[place, row, :]
+        whole_cos = step_cos[place, row, :]
+        whole_sin = step_sin[place, row, :]
         for start in range(0, width, chunk_w):
             lanes = slice(start, start + chunk_w)
-            re = values[half, pl.ds(value_row(pair), 1), lanes]
-            im = values[half, pl.ds(value_row(pair) + 2, 1), lanes]
-            cos = fine_cos[pair, :, lanes]
-            sin = fine_sin[pair, :, lanes]
+            re = whole_re[:, lanes]
+            im = whole_im[:, lanes]
+            cos = fine_cos[pair, place, :, lanes]
+            sin = fine_sin[pair, place, :, lanes]
             real_rows = [re * cos - im * sin]
             imag_rows = [re * sin + im * cos]
-            cos = step_cos[pl.ds(pair_row(pair), 1), lanes]
-            sin = step_sin[pl.ds(pair_row(pair), 1), lanes]
+            cos = jnp.broadcast_to(whole_cos[:, lanes], (8, chunk_w))
+            sin = jnp.broadcast_to(whole_sin[:, lanes], (8, chunk_w))
             for _ in range(blocks_x - 1):
                 re, im = real_rows[-1], imag_rows[-1]
                 real_rows.append(re * cos - im * sin)
@@ -528,25 +583,33 @@
             both = jnp.concatenate([high, low], axis=0)
             total = total + lax.dot_general(
                 both,
-                one_hot(pair, lanes),
+                hot_columns(whole_index[:, lanes]),
                 (((1,), (1,)), ((), ())),
                 preferred_element_type=F32,
             )
-        table[pair] = total[: 2 * side_x] + total[2 * side_x :]
-        return carry
+        total = total[: 2 * side_x] + total[2 * side_x :]
+        table[pair] = total if first else table[pair] + total
 
     for half in range(2):
-        wait_blocks(stokes_in.at[half], n_vis - 1, stokes_recv.at[half])
-
-        def order_stokes(group, carry):
-            lanes = pl.ds(pl.multiple_of(group * 128, 128), 128)
-            blocks = [stokes_in[half, 4 * group + member] for member in range(4)]
-            for turn, rows in enumerate(slots_to_pairs(blocks)):
-                values[half, 4 * turn : 4 * turn + 4, lanes] = rows
-            return carry
-
-        lax.fori_loop(0, n_vis // 4, order_stokes, 0)
-        lax.fori_loop(8 * half, 8 * half + 8, backward_pair, 0)
+        for away in range(2):
+            place = side ^ away
+            count = n_vis // 2 - (1 - away)
+            wait_blocks(stokes_in.at[half], count, stokes_recv.at[half, away])
+
+            def order_stokes(group, carry):
+                lanes = pl.ds(pl.multiple_of(group * 128, 128), 128)
+                first = place * (n_vis // 2) + 4 * group
+                blocks = [stokes_in[half, first + member] for member in range(4)]
+                for turn, rows in enumerate(slots_to_pairs(blocks)):
+                    values[half, place, 4 * turn : 4 * turn + 4, lanes] = rows
+                return carry
+
+            def backward(pair, carry):
+                backward_pair(pair, place, away == 0)
+                return carry
+
+            lax.fori_loop(0, n_vis // 8, order_stokes, 0, unroll=4)
+            lax.fori_loop(8 * half, 8 * half + 8, backward, 0, unroll=8)
 
     wait_blocks(gain_all, n_vis - 1, gain_send)
     for half in range(2):
@@ -586,14 +649,24 @@
             work_im[b, rows, :] = re * sin + im * cos
         return carry
 
-    lax.fori_loop(0, side_x // 8, backward_rows, 0)
+    lax.fori_loop(0, side_x // 8, backward_rows, 0, unroll=8)
 
     last_hi = turn_ref[: 2 * INNER]
     last_lo = turn_ref[2 * INNER :]
-    for b in range(RADIX):
-        high, low = split_pair(jnp.concatenate([work_re[b], work_im[b]], axis=1))
-        part = matmul(high, last_hi) + (matmul(high, last_lo) + matmul(low, last_hi))
-        lines[pl.ds(b, INNER, stride=RADIX), :] = (part * factor).T
+    last_both = jnp.concatenate([last_hi, last_lo], axis=1)
+    group_b = 8
+    for start in range(0, RADIX, group_b):
+        halves = [
+            split_pair(jnp.concatenate([work_re[b], work_im[b]], axis=1))
+            for b in range(start, start + group_b)
+        ]
+        high = jnp.concatenate([pair[0] for pair in halves], axis=0)
+        low = jnp.concatenate([pair[1] for pair in halves], axis=0)
+        both = matmul(high, last_both)
+        part = (both[:, :INNER] + (both[:, INNER:] + matmul(low, last_hi))) * factor
+        for place in range(group_b):
+            here = part[place * side_x : (place + 1) * side_x]
+            lines[pl.ds(start + place, INNER, stride=RADIX), :] = here.T
     count = dirty_sem.shape[0]
     wide = SIDE // count
     copies = []
@@ -625,7 +698,7 @@
     n_facet = lax.axis_size("facet")
     side_x = model_image.shape[1]
     slots = visibilities.shape[1]
-    width = n_vis * slots // RADIX
+    width = n_vis * slots // RADIX // 2
 
     def rows_of(array):
         return array.reshape(-1, 128)
@@ -668,18 +741,19 @@
             pltpu.VMEM((SIDE, side_x), F32),
             work,
             work,
-            pltpu.VMEM((16, width), jnp.int32),
-            pltpu.VMEM((16, width), jnp.int32),
+            pltpu.VMEM((2, 16, width), jnp.int32),
+            pltpu.VMEM((2, 16, width), jnp.int32),
+            pltpu.VMEM((2, 2, 16, width), F32),
             pltpu.VMEM((2, 16, width), F32),
-            pltpu.VMEM((16, width), F32),
-            pltpu.VMEM((16, width), F32),
-            pltpu.VMEM((RADIX, 8, width), F32),
-            pltpu.VMEM((RADIX, 8, width), F32),
+            pltpu.VMEM((2, 16, width), F32),
+            pltpu.VMEM((RADIX, 2, 8, width), F32),
+            pltpu.VMEM((RADIX, 2, 8, width), F32),
             pltpu.SemaphoreType.DMA((len(given),)),
             pltpu.SemaphoreType.DMA(()),
             pltpu.SemaphoreType.DMA(()),
         ]
-        + [pltpu.SemaphoreType.DMA((2,))] * 6,
+        + [pltpu.SemaphoreType.DMA((2,))] * 5
+        + [pltpu.SemaphoreType.DMA((2, 2))],
         compiler_params=pltpu.CompilerParams(
             collective_id=0, has_side_effects=True, vmem_limit_bytes=40 * 1024 * 1024
         ),

time: 44.6 us -> 38.7 us (0.87)
  Pallas kernels: 43.8 us -> 37.9 us
    pallas_call x1, Pallas kernels: 41.7 us -> 36.1 us  [per_device(): pl.pallas_call(functools.partial(exchange_kernel, n_vis, n_facet), out_sh...]
where the time goes in v2:
time: 38.7 us; the launch traced here: 38.6 us
  Pallas kernels  37.9 us (98%)
  between operations  0.64 us (2%)
    pallas_call x1, Pallas kernels, per_device(): pl.pallas_call(functools.partial(exchange_kernel, n_vis, n_facet), out_sh...  36.1 us
    pallas_call x1, Pallas kernels, per_device(): pl.pallas_call(functools.partial(image_kernel, 4.0 / math.sqrt(slots * n_...  1.81 us

profile of v2, /device:TPU:1, one launch (start us, length us, event | category | flops | bytes accessed | tf_op | source)
XLA Modules:
  0.0 38.6 jit_solution(13415453785887056996)
XLA Ops:
  0.6 36.1 %shard_map.131 = (f32[8,512]{1,0:T(8,128)S(1)}, f32[16,128,128]{2,1,0:T(8,128)S(1)}, bf16[512,128]{1,0:T(8,128)(2,1)S(1)}, f32[2,16,128]{2,1,0:T(8,128)S(1)}) custom-call(f32[8,512]{1,0:T(8,128)} %vis_hbm.1, f32[4,128]{1,0:T(4,128)} %bitcast.14, s32[4,128]{1,0:T(4,128)} %bitcast.15, s32[4,128]{1,0:T(4,128)} %bitcast.16, s32[4,128]{1,0:T(4,128)} %bitcast.17, ...), custom_call_target="tpu_custom_call" | custom-call | tf_op jit(solution)/shard_map/pallas_call | solution.py:724
  36.8 1.8 %shard_map.132 = (f32[8,512]{1,0:T(8,128)}, f32[64,2048]{1,0:T(8,128)}) custom-call(f32[8,512]{1,0:T(8,128)S(1)} %get-tuple-element.8.resid_ref, f32[16,128,128]{2,1,0:T(8,128)S(1)} %get-tuple-element.9.table, bf16[512,128]{1,0:T(8,128)(2,1)S(1)} %get-tuple-element.10.turn_ref, f32[2,16,128]{2,1,0:T(8,128)S(1)} %get-tuple-element.11.twist_ref), custom_call_target="tpu_custom_call" | custom-call | tf_op jit(solution)/shard_map/pallas_call | solution.py:761

commit v3 on v2

--- a/solution.py
+++ b/solution.py
@@ -99,10 +99,12 @@
     sine = angle * (
         1.0
         + square
-        * (-1.0 / 6 + square * (1.0 / 120 + square * (-1.0 / 5040 + square * (1.0 / 362880))))
+        * (-1.6666654611e-1 + square * (8.3321608736e-3 + square * -1.9515295891e-4))
     )
     cosine = 1.0 + square * (
-        -0.5 + square * (1.0 / 24 + square * (-1.0 / 720 + square * (1.0 / 40320)))
+        -0.5
+        + square
+        * (4.166664568298827e-2 + square * (-1.388731625493765e-3 + square * 2.443315711809948e-5))
     )
     odd = (quarter & 1) == 1
     cos_mag = jnp.where(odd, sine, cosine)
@@ -360,16 +362,26 @@
         step_cos[place] = cos
         step_sin[place] = sin
 
+    def fine_phases(pair, carry):
+        x_index = me * side_x + lax.broadcasted_iota(jnp.int32, (8, width), 0)
+        for place in range(2):
+            column = local_col[place, pl.ds(pair_row(pair), 1), :]
+            cos, sin = unit_phase((column * x_index) & (SIDE - 1))
+            fine_cos[pair, place] = cos
+            fine_sin[pair, place] = sin
+        return carry
+
+    lax.fori_loop(0, RADIX, fine_phases, 0, unroll=4)
+
     loads[2].wait()
     intervals_here = gain_ref.shape[1]
     stations = gain_ref.shape[2]
-    gain_all[me] = jnp.zeros((8, 256), F32)
+    core, chip = me & 1, me // 2
+    gain_all[core, chip] = jnp.zeros((8, 256), F32)
     for comp in range(8):
         half, lane = comp // 4, 64 * (comp % 4)
-        gain_all[me, 4 * half : 4 * half + intervals_here, lane : lane + stations] = gain_ref[comp]
-
-    pl.semaphore_wait(barrier, n_vis + n_facet - 2)
-    send_all(lambda peer: gain_all.at[me], gain_all, gain_send, lambda step: gain_recv)
+        rows = slice(4 * half, 4 * half + intervals_here)
+        gain_all[core, chip, rows, lane : lane + stations] = gain_ref[comp]
 
     loads[3].wait()
     lines[...] = image_ref[...].T
@@ -407,6 +419,18 @@
 
     lax.fori_loop(0, side_x // 8, forward_rows, 0, unroll=4)
 
+    pl.semaphore_wait(barrier, n_vis + n_facet - 2)
+    for step in vis_steps:
+        if step[2] == 0:
+            pltpu.make_async_remote_copy(
+                src_ref=gain_all.at[core, chip],
+                dst_ref=gain_all.at[core, chip],
+                send_sem=gain_send.at[0],
+                recv_sem=gain_recv.at[0],
+                device_id=(vis_peer(step), facet),
+                device_id_type=MESH,
+            ).start()
+
     chunk_w = 256
     by_lanes = 256
     blocks_x = side_x // 8
@@ -439,13 +463,10 @@
             out_re = []
             out_im = []
             whole_index = local_row[place, row, :]
-            whole_column = local_col[place, row, :]
             whole_cos = step_cos[place, row, :]
             whole_sin = step_sin[place, row, :]
-            x_index = me * side_x + lax.broadcasted_iota(jnp.int32, (8, width), 0)
-            all_cos, all_sin = unit_phase((whole_column * x_index) & (SIDE - 1))
-            fine_cos[pair, place] = all_cos
-            fine_sin[pair, place] = all_sin
+            all_cos = fine_cos[pair, place]
+            all_sin = fine_sin[pair, place]
             for start, size, picker in pieces:
                 lanes = slice(start, start + size)
                 pick = picker(whole_index[:, lanes])
@@ -471,7 +492,7 @@
         return carry
 
     for half in range(2):
-        lax.fori_loop(8 * half, 8 * half + 8, forward_pair, 0, unroll=4)
+        lax.fori_loop(8 * half, 8 * half + 8, forward_pair, 0, unroll=8)
 
         def pack_values(group, carry):
             place, lanes = group_place(group)
@@ -491,11 +512,22 @@
 
     for load in loads[6:]:
         load.wait()
-    wait_blocks(gain_all, n_vis - 1, gain_recv)
+    wait_blocks(gain_all.at[core], n_vis // 2 - 1, gain_recv.at[0])
+    to_other_core = pltpu.make_async_remote_copy(
+        src_ref=gain_all.at[core],
+        dst_ref=gain_all.at[core],
+        send_sem=gain_send.at[1],
+        recv_sem=gain_recv.at[1],
+        device_id=(me ^ 1, facet),
+        device_id_type=MESH,
+    )
+    to_other_core.start()
+    wait_blocks(gain_all.at[1 - core], n_vis // 2, gain_recv.at[1])
     high, low = split_pair(gain_all[...].reshape(n_vis * 8, 256).T)
     both = jnp.concatenate([high, low], axis=0)
     interval = wide_row(interval_ref[...])
-    gain_row = (interval >> 2) * 8 + (interval & 3)
+    holder = interval >> 2
+    gain_row = ((holder & 1) * (n_vis // 2) + (holder >> 1)) * 8 + (interval & 3)
     station = lax.broadcasted_iota(jnp.int32, (64, slots), 0)
     at_p = jnp.where(station == wide_row(station_p_ref[...]), 1.0, 0.0)
     at_q = jnp.where(station == wide_row(station_q_ref[...]), 1.0, 0.0)
@@ -611,7 +643,8 @@
             lax.fori_loop(0, n_vis // 8, order_stokes, 0, unroll=4)
             lax.fori_loop(8 * half, 8 * half + 8, backward, 0, unroll=8)
 
-    wait_blocks(gain_all, n_vis - 1, gain_send)
+    wait_blocks(gain_all.at[core], n_vis // 2 - 1, gain_send.at[0])
+    wait_blocks(gain_all.at[core], n_vis // 2, gain_send.at[1])
     for half in range(2):
         wait_blocks(part_in.at[half], n_vis - 1, part_send.at[half])
         wait_blocks(pred_in.at[half], n_facet - 1, pred_send.at[half])
@@ -733,7 +766,7 @@
         out_specs=(in_vmem,) * 4,
         scratch_shapes=[pltpu.VMEM(array.shape, array.dtype) for array in given[:-2]]
         + [
-            pltpu.VMEM((n_vis, 8, 256), F32),
+            pltpu.VMEM((2, n_vis // 2, 8, 256), F32),
             pltpu.VMEM((2, n_vis, 4, 128), F32),
             pltpu.VMEM((2, n_vis, 4, 128), F32),
             pltpu.VMEM((2, n_facet, 8, slots // 2), F32),
@@ -749,10 +782,8 @@
             pltpu.VMEM((RADIX, 2, 8, width), F32),
             pltpu.VMEM((RADIX, 2, 8, width), F32),
             pltpu.SemaphoreType.DMA((len(given),)),
-            pltpu.SemaphoreType.DMA(()),
-            pltpu.SemaphoreType.DMA(()),
         ]
-        + [pltpu.SemaphoreType.DMA((2,))] * 5
+        + [pltpu.SemaphoreType.DMA((2,))] * 7
         + [pltpu.SemaphoreType.DMA((2, 2))],
         compiler_params=pltpu.CompilerParams(
             collective_id=0, has_side_effects=True, vmem_limit_bytes=40 * 1024 * 1024

time: 38.7 us -> 35.9 us (0.928)
  Pallas kernels: 37.9 us -> 35.1 us
    pallas_call x1, Pallas kernels: 36.1 us -> 33.3 us  [per_device(): pl.pallas_call(functools.partial(exchange_kernel, n_vis, n_facet), out_sh...]
where the time goes in v3:
time: 35.9 us; the launch traced here: 35.8 us
  Pallas kernels  35.1 us (98%)
  between operations  0.64 us (2%)
    pallas_call x1, Pallas kernels, per_device(): pl.pallas_call(functools.partial(exchange_kernel, n_vis, n_facet), out_sh...  33.3 us
    pallas_call x1, Pallas kernels, per_device(): pl.pallas_call(functools.partial(image_kernel, 4.0 / math.sqrt(slots * n_...  1.81 us

profile of v3, /device:TPU:1, one launch (start us, length us, event | category | flops | bytes accessed | tf_op | source)
XLA Modules:
  0.0 35.8 jit_solution(584616571131134038)
XLA Ops:
  0.6 33.3 %shard_map.131 = (f32[8,512]{1,0:T(8,128)S(1)}, f32[16,128,128]{2,1,0:T(8,128)S(1)}, bf16[512,128]{1,0:T(8,128)(2,1)S(1)}, f32[2,16,128]{2,1,0:T(8,128)S(1)}) custom-call(f32[8,512]{1,0:T(8,128)} %vis_hbm.1, f32[4,128]{1,0:T(4,128)} %bitcast.14, s32[4,128]{1,0:T(4,128)} %bitcast.15, s32[4,128]{1,0:T(4,128)} %bitcast.16, s32[4,128]{1,0:T(4,128)} %bitcast.17, ...), custom_call_target="tpu_custom_call" | custom-call | tf_op jit(solution)/shard_map/pallas_call | solution.py:757
  33.9 1.8 %shard_map.132 = (f32[8,512]{1,0:T(8,128)}, f32[64,2048]{1,0:T(8,128)}) custom-call(f32[8,512]{1,0:T(8,128)S(1)} %get-tuple-element.8.resid_ref, f32[16,128,128]{2,1,0:T(8,128)S(1)} %get-tuple-element.9.table, bf16[512,128]{1,0:T(8,128)(2,1)S(1)} %get-tuple-element.10.turn_ref, f32[2,16,128]{2,1,0:T(8,128)S(1)} %get-tuple-element.11.twist_ref), custom_call_target="tpu_custom_call" | custom-call | tf_op jit(solution)/shard_map/pallas_call | solution.py:792

commit v4 on v3

--- a/solution.py
+++ b/solution.py
@@ -17,6 +17,7 @@
 RADIX = 16
 INNER = 128
 SIDE = RADIX * INNER
+PARTS = 2
 
 
 def split_table(table):
@@ -255,6 +256,8 @@
     load_sem,
     gain_send,
     gain_recv,
+    gain_pair_send,
+    gain_pair_recv,
     part_send,
     part_recv,
     pred_send,
@@ -267,7 +270,9 @@
     side_x = image_ref.shape[0]
     width = values.shape[3]
     slots = vis_ref.shape[1]
-    part = slots // 2
+    parts, rows_k = part_in.shape[0], part_in.shape[2] // 2
+    part = slots // parts
+    part_pairs = RADIX // parts
 
     order = (
         (cell_row_hbm, cell_row_ref),
@@ -361,17 +366,6 @@
         cos, sin = unit_phase((local_col[place] * 8) & (SIDE - 1))
         step_cos[place] = cos
         step_sin[place] = sin
-
-    def fine_phases(pair, carry):
-        x_index = me * side_x + lax.broadcasted_iota(jnp.int32, (8, width), 0)
-        for place in range(2):
-            column = local_col[place, pl.ds(pair_row(pair), 1), :]
-            cos, sin = unit_phase((column * x_index) & (SIDE - 1))
-            fine_cos[pair, place] = cos
-            fine_sin[pair, place] = sin
-        return carry
-
-    lax.fori_loop(0, RADIX, fine_phases, 0, unroll=4)
 
     loads[2].wait()
     intervals_here = gain_ref.shape[1]
@@ -426,7 +420,7 @@
                 src_ref=gain_all.at[core, chip],
                 dst_ref=gain_all.at[core, chip],
                 send_sem=gain_send.at[0],
-                recv_sem=gain_recv.at[0],
+                recv_sem=gain_recv.at[step[0]],
                 device_id=(vis_peer(step), facet),
                 device_id_type=MESH,
             ).start()
@@ -440,10 +434,10 @@
         return jnp.where(index == local, 1.0, 0.0).astype(BF16)
 
     def value_row(pair):
-        return lax.rem(pair, 4) * 4 + lax.rem(pair // 4, 2)
+        return lax.rem(pair, 4) * 2 * rows_k + lax.rem(pair // 4, rows_k)
 
     def forward_pair(pair, carry):
-        half = pair // 8
+        half = pair // part_pairs
         row = pl.ds(pair_row(pair), 1)
         high, low = split_pair(table[pair])
         both = jnp.concatenate([high, low], axis=0)
@@ -465,8 +459,10 @@
             whole_index = local_row[place, row, :]
             whole_cos = step_cos[place, row, :]
             whole_sin = step_sin[place, row, :]
-            all_cos = fine_cos[pair, place]
-            all_sin = fine_sin[pair, place]
+            x_index = me * side_x + lax.broadcasted_iota(jnp.int32, (8, width), 0)
+            all_cos, all_sin = unit_phase((local_col[place, row, :] * x_index) & (SIDE - 1))
+            fine_cos[pair, place] = all_cos
+            fine_sin[pair, place] = all_sin
             for start, size, picker in pieces:
                 lanes = slice(start, start + size)
                 pick = picker(whole_index[:, lanes])
@@ -486,17 +482,22 @@
                 out_re.append(jnp.sum(sum_re * cos + sum_im * sin, axis=0, keepdims=True))
                 out_im.append(jnp.sum(sum_im * cos - sum_re * sin, axis=0, keepdims=True))
             re_row = pl.ds(value_row(pair), 1)
-            im_row = pl.ds(value_row(pair) + 2, 1)
+            im_row = pl.ds(value_row(pair) + rows_k, 1)
             values[half, place, re_row, :] = jnp.concatenate(out_re, axis=1)
             values[half, place, im_row, :] = jnp.concatenate(out_im, axis=1)
         return carry
 
-    for half in range(2):
-        lax.fori_loop(8 * half, 8 * half + 8, forward_pair, 0, unroll=8)
+    for half in range(parts):
+        lax.fori_loop(
+            part_pairs * half, part_pairs * (half + 1), forward_pair, 0, unroll=min(8, part_pairs)
+        )
 
         def pack_values(group, carry):
             place, lanes = group_place(group)
-            rows = [values[half, place, 4 * turn : 4 * turn + 4, lanes] for turn in range(4)]
+            rows = [
+                values[half, place, 2 * rows_k * turn : 2 * rows_k * (turn + 1), lanes]
+                for turn in range(4)
+            ]
             for member, block in enumerate(pairs_to_slots(rows)):
                 part_out[half, 4 * group + member] = block
             return carry
@@ -512,19 +513,6 @@
 
     for load in loads[6:]:
         load.wait()
-    wait_blocks(gain_all.at[core], n_vis // 2 - 1, gain_recv.at[0])
-    to_other_core = pltpu.make_async_remote_copy(
-        src_ref=gain_all.at[core],
-        dst_ref=gain_all.at[core],
-        send_sem=gain_send.at[1],
-        recv_sem=gain_recv.at[1],
-        device_id=(me ^ 1, facet),
-        device_id_type=MESH,
-    )
-    to_other_core.start()
-    wait_blocks(gain_all.at[1 - core], n_vis // 2, gain_recv.at[1])
-    high, low = split_pair(gain_all[...].reshape(n_vis * 8, 256).T)
-    both = jnp.concatenate([high, low], axis=0)
     interval = wide_row(interval_ref[...])
     holder = interval >> 2
     gain_row = ((holder & 1) * (n_vis // 2) + (holder >> 1)) * 8 + (interval & 3)
@@ -532,26 +520,47 @@
     at_p = jnp.where(station == wide_row(station_p_ref[...]), 1.0, 0.0)
     at_q = jnp.where(station == wide_row(station_q_ref[...]), 1.0, 0.0)
     index = lax.broadcasted_iota(jnp.int32, (n_vis * 8, slots), 0)
+    hots = [
+        jnp.where(index == gain_row + 4 * half, 1.0, 0.0).astype(BF16) for half in range(2)
+    ]
+    live = wide_row(live_ref[...]).astype(F32)
+    scale = wide_row(weight_ref[...]) * live
+    to_other_core = []
+    for away in range(2):
+        wait_blocks(gain_all.at[core], ring_z - 1 + away, gain_recv.at[away])
+        chips = pl.ds((side ^ away) * ring_z, ring_z)
+        to_other_core.append(
+            pltpu.make_async_remote_copy(
+                src_ref=gain_all.at[core, chips],
+                dst_ref=gain_all.at[core, chips],
+                send_sem=gain_pair_send.at[away],
+                recv_sem=gain_pair_recv.at[away],
+                device_id=(me ^ 1, facet),
+                device_id_type=MESH,
+            )
+        )
+        to_other_core[-1].start()
+    for away in range(2):
+        wait_blocks(gain_all.at[1 - core], ring_z, gain_pair_recv.at[away])
+    high, low = split_pair(gain_all[...].reshape(n_vis * 8, 256).T)
+    both = jnp.concatenate([high, low], axis=0)
     jones_p = []
     jones_q = []
     for half in range(2):
-        hot = jnp.where(index == gain_row + 4 * half, 1.0, 0.0).astype(BF16)
-        picked = matmul(both, hot)
+        picked = matmul(both, hots[half])
         picked = picked[:256] + picked[256:]
         for comp in range(4):
             here = picked[64 * comp : 64 * comp + 64]
             jones_p.append(jnp.sum(here * at_p, axis=0, keepdims=True))
             jones_q.append(jnp.sum(here * at_q, axis=0, keepdims=True))
     outer_re, outer_im = jones_outer(jones_p, jones_q)
-    live = wide_row(live_ref[...]).astype(F32)
-    scale = wide_row(weight_ref[...]) * live
-
-    for half in range(2):
+
+    for half in range(parts):
         here = slice(half * part, (half + 1) * part)
         wait_blocks(part_in.at[half], n_vis - 1, part_recv.at[half])
         model = jnp.sum(part_in[half], axis=0) * (1.0 / SIDE)
-        model_re = wide_row(model[0:2])
-        model_im = wide_row(model[2:4])
+        model_re = wide_row(model[:rows_k])
+        model_im = wide_row(model[rows_k:])
         own_re, own_im = outer_re[:, here], outer_im[:, here]
         pred_in[half, facet, 0:4, :] = model_re * own_re - model_im * own_im
         pred_in[half, facet, 4:8, :] = model_re * own_im + model_im * own_re
@@ -566,7 +575,7 @@
                 device_id_type=MESH,
             ).start()
 
-    for half in range(2):
+    for half in range(parts):
         here = slice(half * part, (half + 1) * part)
         wait_blocks(pred_in.at[half], n_facet - 1, pred_recv.at[half])
         predicted = pred_in[half, 0]
@@ -579,8 +588,8 @@
             [gain[:, here] for gain in jones_q],
             [resid[comp : comp + 1] for comp in range(8)],
         )
-        stokes_in[half, me, 0:2, :] = tall_block(stokes_re * scale[:, here])
-        stokes_in[half, me, 2:4, :] = tall_block(stokes_im * scale[:, here])
+        stokes_in[half, me, :rows_k, :] = tall_block(stokes_re * scale[:, here])
+        stokes_in[half, me, rows_k:, :] = tall_block(stokes_im * scale[:, here])
         send_all(
             lambda peer: stokes_in.at[half, me],
             stokes_in.at[half],
@@ -590,10 +599,10 @@
 
     def backward_pair(pair, place, first):
         total = jnp.zeros((4 * side_x, INNER), F32)
-        half = pair // 8
+        half = pair // part_pairs
         row = pl.ds(pair_row(pair), 1)
         whole_re = values[half, place, pl.ds(value_row(pair), 1), :]
-        whole_im = values[half, place, pl.ds(value_row(pair) + 2, 1), :]
+        whole_im = values[half, place, pl.ds(value_row(pair) + rows_k, 1), :]
         whole_index = local_row[place, row, :]
         whole_cos = step_cos[place, row, :]
         whole_sin = step_sin[place, row, :]
@@ -622,7 +631,7 @@
         total = total[: 2 * side_x] + total[2 * side_x :]
         table[pair] = total if first else table[pair] + total
 
-    for half in range(2):
+    for half in range(parts):
         for away in range(2):
             place = side ^ away
             count = n_vis // 2 - (1 - away)
@@ -633,7 +642,7 @@
                 first = place * (n_vis // 2) + 4 * group
                 blocks = [stokes_in[half, first + member] for member in range(4)]
                 for turn, rows in enumerate(slots_to_pairs(blocks)):
-                    values[half, place, 4 * turn : 4 * turn + 4, lanes] = rows
+                    values[half, place, 2 * rows_k * turn : 2 * rows_k * (turn + 1), lanes] = rows
                 return carry
 
             def backward(pair, carry):
@@ -641,11 +650,14 @@
                 return carry
 
             lax.fori_loop(0, n_vis // 8, order_stokes, 0, unroll=4)
-            lax.fori_loop(8 * half, 8 * half + 8, backward, 0, unroll=8)
+            lax.fori_loop(
+                part_pairs * half, part_pairs * (half + 1), backward, 0, unroll=min(8, part_pairs)
+            )
 
     wait_blocks(gain_all.at[core], n_vis // 2 - 1, gain_send.at[0])
-    wait_blocks(gain_all.at[core], n_vis // 2, gain_send.at[1])
-    for half in range(2):
+    for away in range(2):
+        wait_blocks(gain_all.at[core], ring_z, gain_pair_send.at[away])
+    for half in range(parts):
         wait_blocks(part_in.at[half], n_vis - 1, part_send.at[half])
         wait_blocks(pred_in.at[half], n_facet - 1, pred_send.at[half])
         wait_blocks(stokes_in.at[half], n_vis - 1, stokes_send.at[half])
@@ -767,24 +779,25 @@
         scratch_shapes=[pltpu.VMEM(array.shape, array.dtype) for array in given[:-2]]
         + [
             pltpu.VMEM((2, n_vis // 2, 8, 256), F32),
-            pltpu.VMEM((2, n_vis, 4, 128), F32),
-            pltpu.VMEM((2, n_vis, 4, 128), F32),
-            pltpu.VMEM((2, n_facet, 8, slots // 2), F32),
-            pltpu.VMEM((2, n_vis, 4, 128), F32),
+            pltpu.VMEM((PARTS, n_vis, 8 // PARTS, 128), F32),
+            pltpu.VMEM((PARTS, n_vis, 8 // PARTS, 128), F32),
+            pltpu.VMEM((PARTS, n_facet, 8, slots // PARTS), F32),
+            pltpu.VMEM((PARTS, n_vis, 8 // PARTS, 128), F32),
             pltpu.VMEM((SIDE, side_x), F32),
             work,
             work,
             pltpu.VMEM((2, 16, width), jnp.int32),
             pltpu.VMEM((2, 16, width), jnp.int32),
-            pltpu.VMEM((2, 2, 16, width), F32),
+            pltpu.VMEM((PARTS, 2, 32 // PARTS, width), F32),
             pltpu.VMEM((2, 16, width), F32),
             pltpu.VMEM((2, 16, width), F32),
             pltpu.VMEM((RADIX, 2, 8, width), F32),
             pltpu.VMEM((RADIX, 2, 8, width), F32),
             pltpu.SemaphoreType.DMA((len(given),)),
         ]
-        + [pltpu.SemaphoreType.DMA((2,))] * 7
-        + [pltpu.SemaphoreType.DMA((2, 2))],
+        + [pltpu.SemaphoreType.DMA((2,))] * 4
+        + [pltpu.SemaphoreType.DMA((PARTS,))] * 5
+        + [pltpu.SemaphoreType.DMA((PARTS, 2))],
         compiler_params=pltpu.CompilerParams(
             collective_id=0, has_side_effects=True, vmem_limit_bytes=40 * 1024 * 1024
         ),

time: 35.9 us -> 35.6 us (level)
  no operation moved by 1% of the time
where the time goes in v4:
time: 35.6 us; the launch traced here: 35.5 us
  Pallas kernels  34.9 us (98%)
  between operations  0.64 us (2%)
    pallas_call x1, Pallas kernels, per_device(): pl.pallas_call(functools.partial(exchange_kernel, n_vis, n_facet), out_sh...  33.1 us
    pallas_call x1, Pallas kernels, per_device(): pl.pallas_call(functools.partial(image_kernel, 4.0 / math.sqrt(slots * n_...  1.81 us

profile of v4, /device:TPU:1, one launch (start us, length us, event | category | flops | bytes accessed | tf_op | source)
XLA Modules:
  0.0 35.5 jit_solution(2337600134625176090)
XLA Ops:
  0.6 33.1 %shard_map.131 = (f32[8,512]{1,0:T(8,128)S(1)}, f32[16,128,128]{2,1,0:T(8,128)S(1)}, bf16[512,128]{1,0:T(8,128)(2,1)S(1)}, f32[2,16,128]{2,1,0:T(8,128)S(1)}) custom-call(f32[8,512]{1,0:T(8,128)} %vis_hbm.1, f32[4,128]{1,0:T(4,128)} %bitcast.14, s32[4,128]{1,0:T(4,128)} %bitcast.15, s32[4,128]{1,0:T(4,128)} %bitcast.16, s32[4,128]{1,0:T(4,128)} %bitcast.17, ...), custom_call_target="tpu_custom_call" | custom-call | tf_op jit(solution)/shard_map/pallas_call | solution.py:769
  33.7 1.8 %shard_map.132 = (f32[8,512]{1,0:T(8,128)}, f32[64,2048]{1,0:T(8,128)}) custom-call(f32[8,512]{1,0:T(8,128)S(1)} %get-tuple-element.8.resid_ref, f32[16,128,128]{2,1,0:T(8,128)S(1)} %get-tuple-element.9.table, bf16[512,128]{1,0:T(8,128)(2,1)S(1)} %get-tuple-element.10.turn_ref, f32[2,16,128]{2,1,0:T(8,128)S(1)} %get-tuple-element.11.twist_ref), custom_call_target="tpu_custom_call" | custom-call | tf_op jit(solution)/shard_map/pallas_call | solution.py:805

commit v5 on v4

--- a/solution.py
+++ b/solution.py
@@ -296,7 +296,8 @@
         load.start()
 
     ring_z, ring_y = n_vis // 4, n_facet // 2
-    side = me // (2 * ring_z)
+    side, own_z, own_core = me // (2 * ring_z), (me // 2) & (ring_z - 1), me & 1
+    own_y, own_x = facet // 2, facet & 1
     vis_steps = [
         (away, along, core)
         for away in range(2)
@@ -310,12 +311,13 @@
 
     def vis_peer(step):
         away, along, core = step
-        z = lax.rem(me // 2 + along, ring_z)
-        return ((side ^ away) * ring_z + z) * 2 + ((me & 1) ^ core)
+        z = (own_z + along) & (ring_z - 1) if along else own_z
+        return ((side ^ away) * ring_z + z) * 2 + (own_core ^ core)
 
     def facet_peer(step):
         along, away = step
-        return lax.rem(facet // 2 + along, ring_y) * 2 + ((facet & 1) ^ away)
+        y = (own_y + along) & (ring_y - 1) if along else own_y
+        return y * 2 + (own_x ^ away)
 
     barrier = pltpu.get_barrier_semaphore()
     for step in vis_steps:
@@ -425,7 +427,7 @@
                 device_id_type=MESH,
             ).start()
 
-    chunk_w = 256
+    chunk_w = 512
     by_lanes = 256
     blocks_x = side_x // 8
 

time: 35.6 us -> 35.6 us (level)
  no operation moved by 1% of the time
where the time goes in v5:
time: 35.6 us; the launch traced here: 35.5 us
  Pallas kernels  34.9 us (98%)
  between operations  0.64 us (2%)
    pallas_call x1, Pallas kernels, per_device(): pl.pallas_call(functools.partial(exchange_kernel, n_vis, n_facet), out_sh...  33.1 us
    pallas_call x1, Pallas kernels, per_device(): pl.pallas_call(functools.partial(image_kernel, 4.0 / math.sqrt(slots * n_...  1.81 us

profile of v5, /device:TPU:1, one launch (start us, length us, event | category | flops | bytes accessed | tf_op | source)
XLA Modules:
  0.0 35.5 jit_solution(14706535628999717504)
XLA Ops:
  0.6 33.1 %shard_map.131 = (f32[8,512]{1,0:T(8,128)S(1)}, f32[16,128,128]{2,1,0:T(8,128)S(1)}, bf16[512,128]{1,0:T(8,128)(2,1)S(1)}, f32[2,16,128]{2,1,0:T(8,128)S(1)}) custom-call(f32[8,512]{1,0:T(8,128)} %vis_hbm.1, f32[4,128]{1,0:T(4,128)} %bitcast.14, s32[4,128]{1,0:T(4,128)} %bitcast.15, s32[4,128]{1,0:T(4,128)} %bitcast.16, s32[4,128]{1,0:T(4,128)} %bitcast.17, ...), custom_call_target="tpu_custom_call" | custom-call | tf_op jit(solution)/shard_map/pallas_call | solution.py:771
  33.7 1.8 %shard_map.132 = (f32[8,512]{1,0:T(8,128)}, f32[64,2048]{1,0:T(8,128)}) custom-call(f32[8,512]{1,0:T(8,128)S(1)} %get-tuple-element.8.resid_ref, f32[16,128,128]{2,1,0:T(8,128)S(1)} %get-tuple-element.9.table, bf16[512,128]{1,0:T(8,128)(2,1)S(1)} %get-tuple-element.10.turn_ref, f32[2,16,128]{2,1,0:T(8,128)S(1)} %get-tuple-element.11.twist_ref), custom_call_target="tpu_custom_call" | custom-call | tf_op jit(solution)/shard_map/pallas_call | solution.py:807
